TPU v7x, 32 devices: a whole 2x2x4 slice. The times are simulated.
32 devices in a mesh: batch: 4 (over y, x), seq: 8 (over z, core).
Axes of the slice: x: 2, y: 2, z: 4, core: 2. Of those that a mesh axis runs over, the one named last changes fastest.
Arguments:
- inputs: bfloat16 [4, 16384, 512], P('batch', 'seq'), may hold values from -6 to 6
- out_grad: bfloat16 [4, 16384, 512], P('batch', 'seq'), may hold values from -6 to 6
- lengths: int32 [4], P('batch'), may hold values from 128 to 16384, as said below
- qkv_weight: float32 [512, 1536], P(('batch', 'seq')), may hold values from -0.125 to 0.125
- proj_weight: float32 [512, 512], P(('batch', 'seq')), may hold values from -3 to 3
- up_weight: float32 [512, 2048], P(('batch', 'seq')), may hold values from -0.125 to 0.125
- down_weight: float32 [2048, 512], P(('batch', 'seq')), may hold values from -0.125 to 0.125
- norm_params: float32 [4, 512], P(None, ('batch', 'seq'))
- qkv_mean: float32 [512, 1536], P(('batch', 'seq')), may hold values from -0.0034179688 to 0.0034179688
- proj_mean: float32 [512, 512], P(('batch', 'seq')), may hold values from -0.0007324219 to 0.0007324219
- up_mean: float32 [512, 2048], P(('batch', 'seq')), may hold values from -0.0007324219 to 0.0007324219
- down_mean: float32 [2048, 512], P(('batch', 'seq')), may hold values from -0.0004272461 to 0.0004272461
- norm_mean: float32 [4, 512], P(None, ('batch', 'seq')), may hold values from -0.009765625 to 0.009765625
- qkv_second: float32 [512, 1536], P(('batch', 'seq')), may hold values from 3.1768462e-07 to 1.2707385e-06
- proj_second: float32 [512, 512], P(('batch', 'seq')), may hold values from 1.588423e-08 to 6.353692e-08
- up_second: float32 [512, 2048], P(('batch', 'seq')), may hold values from 1.588423e-08 to 6.353692e-08
- down_second: float32 [2048, 512], P(('batch', 'seq')), may hold values from 4.9638222e-09 to 1.9855289e-08
- norm_second: float32 [4, 512], P(None, ('batch', 'seq')), may hold values from 2.8591614e-06 to 1.1436646e-05
Outputs:
- outputs: bfloat16 [4, 16384, 512], P('batch', 'seq')
- input_grad: float32 [4, 16384, 512], P('batch', 'seq')
- grad_norm: float32 [], replicated
- qkv_moment: float32 [512, 1536], P(('batch', 'seq'))
- proj_moment: float32 [512, 512], P(('batch', 'seq'))
- up_moment: float32 [512, 2048], P(('batch', 'seq'))
- down_moment: float32 [2048, 512], P(('batch', 'seq'))
- norm_moment: float32 [4, 512], P(None, ('batch', 'seq'))
- qkv_square: float32 [512, 1536], P(('batch', 'seq'))
- proj_square: float32 [512, 512], P(('batch', 'seq'))
- up_square: float32 [512, 2048], P(('batch', 'seq'))
- down_square: float32 [2048, 512], P(('batch', 'seq'))
- norm_square: float32 [4, 512], P(None, ('batch', 'seq'))
- qkv_master: float32 [512, 1536], P(('batch', 'seq'))
- proj_master: float32 [512, 512], P(('batch', 'seq'))
- up_master: float32 [512, 2048], P(('batch', 'seq'))
- down_master: float32 [2048, 512], P(('batch', 'seq'))
- norm_master: float32 [4, 512], P(None, ('batch', 'seq'))
- shift_clipped: float32 [512], P(('batch', 'seq'))
Inputs may be any that keep to these rules, and one draw needn't show every extreme that they name: `lengths`: one of the 4 sequences in every draw has all 16384 tokens.
All inputs are finite; a program needn't handle non-finite values.
Results may differ from a plain program's by a relative error of at most 0.012.
The roundings to bfloat16 on the way count: a program that leaves them out, or rounds other values in their place, can miss the bound.
Values may be sent and summed in bfloat16 or wider, within the bound.
A program may use at most 384 MiB of HBM per device.

v0:
```python
import jax
import jax.numpy as jnp
from jax import lax
from jax.sharding import PartitionSpec as P

HEADS = 8
HD = 64
SPAN = 128
STEP = 10


LN_EPS = 1e-05
NEG_FILL = -1e30
CLIP = 1.0
BETA = 0.5
ADAM_EPS = 1e-08
DECAY = 0.1
RATES = (0.02, 0.3, 0.02, 0.02, 0.5)


def layer_norm(vector, gain, shift):
    centre = jnp.mean(vector, axis=-1, keepdims=True)
    centred = vector - centre
    spread = jnp.mean(centred * centred, axis=-1, keepdims=True)
    return centred * lax.rsqrt(spread + LN_EPS) * gain + shift


def regroup(grad, dim, outer, inner):
    shape = grad.shape
    piece = shape[dim] // (outer * inner)
    split = grad.reshape(shape[:dim] + (outer, inner, piece) + shape[dim + 1 :])
    return jnp.swapaxes(split, dim, dim + 1).reshape(shape)


def scores_for(query_b, keys_b, summ_keys, key_ok, span_index, summ_ok):
    spans = query_b.shape[0]
    near = (
        jnp.einsum("sqhd,skhd->shqk", query_b, keys_b, preferred_element_type=jnp.float32) * 0.125
    )
    far = (
        jnp.einsum("sqhd,nhd->shqn", query_b, summ_keys, preferred_element_type=jnp.float32) * 0.125
    )
    causal = lax.broadcasted_iota(jnp.int32, (SPAN, SPAN), 0) >= lax.broadcasted_iota(
        jnp.int32, (SPAN, SPAN), 1
    )
    near_ok = causal[None, None] & key_ok[:, None, None, :]
    far_ok = (
        lax.broadcasted_iota(jnp.int32, (spans, summ_keys.shape[0]), 1) < span_index[:, None]
    ) & summ_ok[None, :]
    near = jnp.where(near_ok, near, NEG_FILL)
    far = jnp.where(far_ok[:, None, None, :], far, NEG_FILL)
    peak = jnp.maximum(jnp.max(near, axis=-1), jnp.max(far, axis=-1))[..., None]
    near_exp = jnp.exp(near - peak)
    far_exp = jnp.exp(far - peak)
    total = jnp.sum(near_exp, axis=-1, keepdims=True) + jnp.sum(far_exp, axis=-1, keepdims=True)
    return (near_exp / total, far_exp / total)


def body(
    inputs,
    out_grad,
    lengths,
    qkv_weight,
    proj_weight,
    up_weight,
    down_weight,
    norm_params,
    qkv_mean,
    proj_mean,
    up_mean,
    down_mean,
    norm_mean,
    qkv_second,
    proj_second,
    up_second,
    down_second,
    norm_second,
):
    qkv_copy = qkv_weight.astype(jnp.bfloat16)
    proj_copy = proj_weight.astype(jnp.bfloat16)
    up_copy = up_weight.astype(jnp.bfloat16)
    down_copy = down_weight.astype(jnp.bfloat16)
    norm_copy = norm_params.astype(jnp.bfloat16)
    qkv_full, proj_full, up_full, down_full, norm_full = (
        lax.all_gather(qkv_copy, ("batch", "seq"), axis=0, tiled=True),
        lax.all_gather(proj_copy, ("batch", "seq"), axis=0, tiled=True),
        lax.all_gather(up_copy, ("batch", "seq"), axis=0, tiled=True),
        lax.all_gather(down_copy, ("batch", "seq"), axis=0, tiled=True),
        lax.all_gather(norm_copy, ("batch", "seq"), axis=1, tiled=True),
    )
    norm_vals = norm_full.astype(jnp.float32)
    rows = inputs.shape[1]
    width = inputs.shape[2]
    seq_index = lax.axis_index("seq")
    local_spans = rows // SPAN
    all_spans = local_spans * lax.axis_size("seq")
    length = lengths[0]
    positions = seq_index * rows + jnp.arange(rows, dtype=jnp.int32)
    key_valid = positions < length
    span_starts = jnp.arange(all_spans, dtype=jnp.int32) * SPAN
    span_counts = jnp.clip(length - span_starts, 0, SPAN)
    summ_ok = span_counts > 0
    span_scale = lax.rsqrt(jnp.maximum(span_counts, 1).astype(jnp.float32))
    own_scale = lax.dynamic_slice_in_dim(span_scale, seq_index * local_spans, local_spans, 0)
    mask_rows = key_valid.reshape(local_spans, SPAN)
    residual_in = inputs[0].astype(jnp.float32)
    normed_one = layer_norm(residual_in, norm_vals[0], norm_vals[1]).astype(jnp.bfloat16)
    mixed = jnp.dot(normed_one, qkv_full, preferred_element_type=jnp.float32).astype(jnp.bfloat16)
    query = mixed[:, :width]
    keys = mixed[:, width : 2 * width]
    values = mixed[:, 2 * width :]
    mask_low = mask_rows.astype(jnp.bfloat16)
    key_sum = jnp.einsum(
        "sp,spd->sd",
        mask_low,
        keys.reshape(local_spans, SPAN, width),
        preferred_element_type=jnp.float32,
    )
    value_sum = jnp.einsum(
        "sp,spd->sd",
        mask_low,
        values.reshape(local_spans, SPAN, width),
        preferred_element_type=jnp.float32,
    )
    own_keys = (key_sum * own_scale[:, None]).astype(jnp.bfloat16)
    own_values = (value_sum * own_scale[:, None]).astype(jnp.bfloat16)
    summ_flat_keys, summ_flat_values = (
        lax.all_gather(own_keys, "seq", axis=0, tiled=True),
        lax.all_gather(own_values, "seq", axis=0, tiled=True),
    )
    summ_keys = summ_flat_keys.reshape(all_spans, HEADS, HD)
    summ_values = summ_flat_values.reshape(all_spans, HEADS, HD)
    block_rows = min(512, rows)
    block_spans = block_rows // SPAN
    block_count = rows // block_rows
    shape = (block_spans, SPAN, HEADS, HD)

    def block_pieces(block_index):
        begin = block_index * block_rows
        ending = begin + block_rows
        span_index = (
            seq_index * local_spans
            + block_index * block_spans
            + jnp.arange(block_spans, dtype=jnp.int32)
        )
        return (
            query[begin:ending].reshape(shape),
            keys[begin:ending].reshape(shape),
            values[begin:ending].reshape(shape),
            mask_rows[block_index * block_spans : (block_index + 1) * block_spans],
            span_index,
        )

    attn_parts = []
    for block_index in range(block_count):
        query_b, keys_b, values_b, okay_b, span_index = block_pieces(block_index)
        near_p, far_p = scores_for(query_b, keys_b, summ_keys, okay_b, span_index, summ_ok)
        mixed_out = jnp.einsum(
            "shqk,skhd->sqhd",
            near_p.astype(jnp.bfloat16),
            values_b,
            preferred_element_type=jnp.float32,
        )
        mixed_out = mixed_out + jnp.einsum(
            "shqn,nhd->sqhd",
            far_p.astype(jnp.bfloat16),
            summ_values,
            preferred_element_type=jnp.float32,
        )
        attn_parts.append(mixed_out.reshape(block_rows, width))
    attn_out = jnp.concatenate(attn_parts, axis=0).astype(jnp.bfloat16)
    resid = residual_in + jnp.dot(attn_out, proj_full, preferred_element_type=jnp.float32)
    normed_two = layer_norm(resid, norm_vals[2], norm_vals[3]).astype(jnp.bfloat16)
    pre_act = jnp.dot(normed_two, up_full, preferred_element_type=jnp.float32)
    activ = jax.nn.gelu(pre_act, approximate=True).astype(jnp.bfloat16)
    outputs = resid + jnp.dot(activ, down_full, preferred_element_type=jnp.float32)
    qkv_back, proj_back, up_back, down_back = (
        lax.all_gather(qkv_copy, ("batch", "seq"), axis=0, tiled=True),
        lax.all_gather(proj_copy, ("batch", "seq"), axis=0, tiled=True),
        lax.all_gather(up_copy, ("batch", "seq"), axis=0, tiled=True),
        lax.all_gather(down_copy, ("batch", "seq"), axis=0, tiled=True),
    )
    grad_rows = out_grad[0]
    down_grad = jnp.einsum("tf,td->fd", activ, grad_rows, preferred_element_type=jnp.float32)
    act_grad = jnp.einsum("td,fd->tf", grad_rows, down_back, preferred_element_type=jnp.float32)
    gelu_pull = jax.vjp(lambda value: jax.nn.gelu(value, approximate=True), pre_act)[1]
    pre_grad = gelu_pull(act_grad)[0].astype(jnp.bfloat16)
    up_grad = jnp.einsum("td,tf->df", normed_two, pre_grad, preferred_element_type=jnp.float32)
    normed_two_grad = jnp.einsum("tf,df->td", pre_grad, up_back, preferred_element_type=jnp.float32)
    norm_pull_two = jax.vjp(layer_norm, resid, norm_vals[2], norm_vals[3])[1]
    resid_part, gain_two_grad, shift_two_grad = norm_pull_two(normed_two_grad)
    resid_grad = grad_rows.astype(jnp.float32) + resid_part
    proj_in_grad = resid_grad.astype(jnp.bfloat16)
    proj_grad = jnp.einsum("td,te->de", attn_out, proj_in_grad, preferred_element_type=jnp.float32)
    attn_grad = jnp.einsum(
        "te,de->td", proj_in_grad, proj_back, preferred_element_type=jnp.float32
    ).astype(jnp.bfloat16)
    summ_key_grad = jnp.zeros((all_spans, HEADS, HD), jnp.float32)
    summ_value_grad = jnp.zeros((all_spans, HEADS, HD), jnp.float32)
    query_parts, key_parts, value_parts = ([], [], [])
    for block_index in range(block_count):
        query_b, keys_b, values_b, okay_b, span_index = block_pieces(block_index)
        near_p, far_p = scores_for(query_b, keys_b, summ_keys, okay_b, span_index, summ_ok)
        near_low = near_p.astype(jnp.bfloat16)
        far_low = far_p.astype(jnp.bfloat16)
        grad_b = attn_grad[block_index * block_rows : (block_index + 1) * block_rows].reshape(shape)
        near_dp = jnp.einsum(
            "sqhd,skhd->shqk", grad_b, values_b, preferred_element_type=jnp.float32
        )
        far_dp = jnp.einsum(
            "sqhd,nhd->shqn", grad_b, summ_values, preferred_element_type=jnp.float32
        )
        row_delta = (jnp.sum(near_dp * near_p, axis=-1) + jnp.sum(far_dp * far_p, axis=-1))[
            ..., None
        ]
        near_ds = (near_p * (near_dp - row_delta)).astype(jnp.bfloat16)
        far_ds = (far_p * (far_dp - row_delta)).astype(jnp.bfloat16)
        query_grad = jnp.einsum(
            "shqk,skhd->sqhd", near_ds, keys_b, preferred_element_type=jnp.float32
        )
        query_grad = (
            query_grad
            + jnp.einsum("shqn,nhd->sqhd", far_ds, summ_keys, preferred_element_type=jnp.float32)
        ) * 0.125
        keys_grad = (
            jnp.einsum("shqk,sqhd->skhd", near_ds, query_b, preferred_element_type=jnp.float32)
            * 0.125
        )
        values_grad = jnp.einsum(
            "shqk,sqhd->skhd", near_low, grad_b, preferred_element_type=jnp.float32
        )
        summ_key_grad = (
            summ_key_grad
            + jnp.einsum("shqn,sqhd->nhd", far_ds, query_b, preferred_element_type=jnp.float32)
            * 0.125
        )
        summ_value_grad = summ_value_grad + jnp.einsum(
            "shqn,sqhd->nhd", far_low, grad_b, preferred_element_type=jnp.float32
        )
        query_parts.append(query_grad.reshape(block_rows, width))
        key_parts.append(keys_grad.reshape(block_rows, width))
        value_parts.append(values_grad.reshape(block_rows, width))
    own_key_grad, own_value_grad = (
        lax.psum_scatter(
            summ_key_grad.reshape(all_spans, width), "seq", scatter_dimension=0, tiled=True
        ),
        lax.psum_scatter(
            summ_value_grad.reshape(all_spans, width), "seq", scatter_dimension=0, tiled=True
        ),
    )
    mask_float = mask_rows.astype(jnp.float32)[:, :, None]
    key_extra = ((own_key_grad * own_scale[:, None])[:, None, :] * mask_float).reshape(rows, width)
    value_extra = ((own_value_grad * own_scale[:, None])[:, None, :] * mask_float).reshape(
        rows, width
    )
    mixed_grad = jnp.concatenate(
        [
            jnp.concatenate(query_parts, axis=0),
            jnp.concatenate(key_parts, axis=0) + key_extra,
            jnp.concatenate(value_parts, axis=0) + value_extra,
        ],
        axis=1,
    ).astype(jnp.bfloat16)
    qkv_grad = jnp.einsum("td,te->de", normed_one, mixed_grad, preferred_element_type=jnp.float32)
    normed_one_grad = jnp.einsum(
        "te,de->td", mixed_grad, qkv_back, preferred_element_type=jnp.float32
    )
    norm_pull_one = jax.vjp(layer_norm, residual_in, norm_vals[0], norm_vals[1])[1]
    input_part, gain_one_grad, shift_one_grad = norm_pull_one(normed_one_grad)
    input_grad = resid_grad + input_part
    norm_grad = jnp.stack([gain_one_grad, shift_one_grad, gain_two_grad, shift_two_grad])
    groups = lax.axis_size("batch")
    seq_count = lax.axis_size("seq")
    sectioned = (
        lax.psum_scatter(
            regroup(qkv_grad, 0, groups, seq_count), "seq", scatter_dimension=0, tiled=True
        ),
        lax.psum_scatter(
            regroup(proj_grad, 0, groups, seq_count), "seq", scatter_dimension=0, tiled=True
        ),
        lax.psum_scatter(
            regroup(up_grad, 0, groups, seq_count), "seq", scatter_dimension=0, tiled=True
        ),
        lax.psum_scatter(
            regroup(down_grad, 0, groups, seq_count), "seq", scatter_dimension=0, tiled=True
        ),
        lax.psum_scatter(
            regroup(norm_grad, 1, groups, seq_count), "seq", scatter_dimension=1, tiled=True
        ),
    )
    reduced = (
        lax.psum_scatter(sectioned[0], "batch", scatter_dimension=0, tiled=True),
        lax.psum_scatter(sectioned[1], "batch", scatter_dimension=0, tiled=True),
        lax.psum_scatter(sectioned[2], "batch", scatter_dimension=0, tiled=True),
        lax.psum_scatter(sectioned[3], "batch", scatter_dimension=0, tiled=True),
        lax.psum_scatter(sectioned[4], "batch", scatter_dimension=1, tiled=True),
    )
    local_squares = sum((jnp.sum(grad * grad) for grad in reduced))
    grad_norm = jnp.sqrt(lax.psum(local_squares, ("batch", "seq")))
    factor = jnp.minimum(1.0, CLIP / (grad_norm + 1e-06))
    fix = 1.0 - BETA**STEP
    masters = (qkv_weight, proj_weight, up_weight, down_weight, norm_params)
    firsts = (qkv_mean, proj_mean, up_mean, down_mean, norm_mean)
    seconds = (qkv_second, proj_second, up_second, down_second, norm_second)
    moments, squares, fresh = ([], [], [])
    for grad, master, first, second, rate in zip(reduced, masters, firsts, seconds, RATES):
        clipped = grad * factor
        moment = BETA * first + (1.0 - BETA) * clipped
        square = BETA * second + (1.0 - BETA) * clipped * clipped
        update = moment / fix / (jnp.sqrt(square / fix) + ADAM_EPS)
        moments.append(moment)
        squares.append(square)
        fresh.append(master - rate * (update + DECAY * master))
    shift_clipped = reduced[4][3] * factor
    return (
        outputs.astype(jnp.bfloat16)[None],
        input_grad[None],
        grad_norm,
        moments[0],
        moments[1],
        moments[2],
        moments[3],
        moments[4],
        squares[0],
        squares[1],
        squares[2],
        squares[3],
        squares[4],
        fresh[0],
        fresh[1],
        fresh[2],
        fresh[3],
        fresh[4],
        shift_clipped,
    )


def solution(mesh):
    return jax.shard_map(
        body,
        mesh=mesh,
        in_specs=(
            P("batch", "seq", None),
            P("batch", "seq", None),
            P("batch"),
            P(("batch", "seq"), None),
            P(("batch", "seq"), None),
            P(("batch", "seq"), None),
            P(("batch", "seq"), None),
            P(None, ("batch", "seq")),
            P(("batch", "seq"), None),
            P(("batch", "seq"), None),
            P(("batch", "seq"), None),
            P(("batch", "seq"), None),
            P(None, ("batch", "seq")),
            P(("batch", "seq"), None),
            P(("batch", "seq"), None),
            P(("batch", "seq"), None),
            P(("batch", "seq"), None),
            P(None, ("batch", "seq")),
        ),
        out_specs=(
            P("batch", "seq", None),
            P("batch", "seq", None),
            P(),
            P(("batch", "seq"), None),
            P(("batch", "seq"), None),
            P(("batch", "seq"), None),
            P(("batch", "seq"), None),
            P(None, ("batch", "seq")),
            P(("batch", "seq"), None),
            P(("batch", "seq"), None),
            P(("batch", "seq"), None),
            P(("batch", "seq"), None),
            P(None, ("batch", "seq")),
            P(("batch", "seq"), None),
            P(("batch", "seq"), None),
            P(("batch", "seq"), None),
            P(("batch", "seq"), None),
            P(None, ("batch", "seq")),
            P(("batch", "seq")),
        ),
        check_vma=False,
    )
```

profile of v0, /device:TPU:0, one launch (start us, length us, event | category | flops | bytes accessed | tf_op | source)
XLA Modules:
  0.0 829.3 jit_solution(8453481967665152769)
XLA Ops:
  14.9 43.3 %all-gather = bf16[32,16,4]{1,2,0:T(4,128)(2,1)S(1)} all-gather(bf16[1,16,4]{1,2,0:T(4,128)(2,1)S(1)} %convert_bitcast_fusion.2), channel_id=1, replica_groups=mesh['batch'=4,'seq'=8] {'batch','seq'}, dimensions={0}, use_global_device_ids=true | all-gather | bytes 4224 | tf_op jit(solution)/shard_map/all_gather | solution.py:89
  59.1 41.9 %all_gather.29 = bf16[512,512]{1,0:T(8,128)(2,1)} all-gather(bf16[16,512]{1,0:T(8,128)(2,1)S(1)} %convert_element_type.147), channel_id=1, replica_groups=mesh['batch'=4,'seq'=8] {'batch','seq'}, dimensions={0}, use_global_device_ids=true | all-gather | bytes 540672 | tf_op jit(solution)/shard_map/all_gather | solution.py:86
  104.9 4.0 copy.685
  112.7 5.8 convolution_convert_fusion
  126.1 14.0 %all_gather.28 = bf16[128,512]{1,0:T(8,128)(2,1)S(1)} all-gather(bf16[16,512]{1,0:T(8,128)(2,1)S(1)} %get-tuple-element.199), channel_id=1, replica_groups=mesh['batch'=4,'seq'=8] {'seq'}, dimensions={0}, use_global_device_ids=true | all-gather | bytes 147456 | tf_op jit(solution)/shard_map/all_gather | solution.py:129
  140.2 15.2 %all_gather.27 = bf16[128,512]{1,0:T(8,128)(2,1)} all-gather(bf16[16,512]{1,0:T(8,128)(2,1)S(1)} %get-tuple-element.200), channel_id=1, replica_groups=mesh['batch'=4,'seq'=8] {'seq'}, dimensions={0}, use_global_device_ids=true | all-gather | bytes 147456 | tf_op jit(solution)/shard_map/all_gather | solution.py:128
  230.7 15.5 %fusion.14 = (bf16[2048,2048]{1,0:T(8,128)(2,1)}, f32[2048,2048]{0,1:T(8,128)}) fusion(bf16[512,2048]{1,0:T(8,128)(2,1)} %all-gather.7.cloned.1.call-done, f32[2048,512]{0,1:T(8,128)} %copy-done.2, f32[512]{0:T(512)S(1)} %bitcast.492, f32[512]{0:T(512)S(1)} %bitcast.487, f32[2048]{0:T(1024)S(1)} %fusion.175, f32[2048]{0:T(1024)S(1)} %broadcast_multiply_fusion.2), kind=kOutput, calls=%fused_computation.17 | convolution fusion | flops 4337958912 | bytes 31477760 | tf_op jit(solution)/shard_map/dot_general | solution.py:174
  246.2 17.8 %copy.683 = f32[2048,2048]{1,0:T(8,128)} copy(f32[2048,2048]{0,1:T(8,128)} %get-tuple-element.224) | data formatting | bytes 33554432 | tf_op jit(solution)/shard_map/dot_general | solution.py:174
  264.0 16.5 %fusion.6 = bf16[2048,2048]{1,0:T(8,128)(2,1)S(1)} fusion(f32[2048,2048]{1,0:T(8,128)} %copy.683, bf16[2048,512]{1,0:T(8,128)(2,1)} %all-gather.9.cloned.1.call-done, bf16[1,2048,512]{2,1,0:T(8,128)(2,1)S(1)} %copy-done.75), kind=kOutput, calls=%fused_computation.9 | convolution fusion | flops 4378853376 | bytes 29360128 | tf_op jit(solution)/shard_map/td,fd->tf/dot_general | solution.py:185
  280.5 7.0 fusion.216
  287.5 5.7 copy.687
  293.2 5.4 multiply_reduce_fusion
  374.8 5.8 fusion.49
  406.3 4.4 fusion.46
  448.0 7.0 reduce-scatter.35.cloned.1.call-done
  466.2 8.5 %fusion.191 = f32[512,2048]{1,0:T(8,128)S(1)} fusion(bf16[2048,2048]{1,0:T(8,128)(2,1)} %copy-done.172, f32[2048,512]{0,1:T(8,128)} %copy-done.2, f32[512]{0:T(512)S(1)} %bitcast.493, f32[512]{0:T(512)S(1)} %bitcast.490, f32[2048]{0:T(1024)S(1)} %copy-done.147, f32[2048]{0:T(1024)S(1)} %copy-done.139), kind=kOutput, calls=%fused_computation.339 | convolution fusion | flops 4300210176 | bytes 16797696 | tf_op jit(solution)/shard_map/td,tf->df/dot_general | solution.py:188
  478.8 6.9 convolution_bitcast_fusion
  490.2 12.5 %fusion.217 = (f32[512]{0:T(512)S(1)}, f32[2048,512]{1,0:T(8,128)}) fusion(bf16[512,1536]{1,0:T(8,128)(2,1)} %all-gather.5.cloned.1.call-done, bf16[2048,512]{1,0:T(8,128)(2,1)} %copy-done.88, bf16[2048,512]{1,0:T(8,128)(2,1)S(1)} %copy-done.87, bf16[512,512]{1,0:T(8,128)(2,1)S(1)} %copy-done.97, bf16[512,512]{1,0:T(8,128)(2,1)S(1)} %copy-done.99, ...), kind=kOutput, calls=%fused_computation.352 | convolution fusion | flops 3260022272 | bytes 12060672 | tf_op jit(solution)/shard_map/te,de->td/dot_general | solution.py:265
  502.8 5.5 copy.778
  515.5 13.1 %reduce-scatter.19.cloned.1.call-done = f32[64,1536]{1,0:T(8,128)} async-done(((f32[512,1536]{1,0:T(8,128)}), f32[64,1536]{1,0:T(8,128)}) %reduce-scatter.19.cloned.1.call-update) | async-done | bytes 393232 | tf_op jit(solution)/shard_map/reduce_scatter | solution.py:275
  529.9 50.1 %reduce-scatter.27.cloned.1.call-done = f32[64,2048]{1,0:T(8,128)} async-done(((f32[512,2048]{1,0:T(8,128)}), f32[64,2048]{1,0:T(8,128)}) %reduce-scatter.27.cloned.1.call-update) | async-done | bytes 524304 | tf_op jit(solution)/shard_map/reduce_scatter | solution.py:281
  580.1 12.7 %fusion.36 = bf16[1,2048,512]{1,2,0:T(8,128)(2,1)} fusion(f32[2048,512]{0,1:T(8,128)} %copy-done.2, bf16[2048,512]{1,0:T(8,128)(2,1)} %all-gather.9.cloned.1.call-done, f32[2048,2048]{1,0:T(8,128)} %copy.683), kind=kOutput, calls=%fused_computation.56 | convolution fusion | flops 4334813184 | bytes 25165824 | tf_op jit(solution)/shard_map/dot_general | solution.py:176
  596.7 33.8 %reduce-scatter.31.cloned.1.call-done = f32[256,512]{1,0:T(8,128)} async-done(((f32[2048,512]{1,0:T(8,128)}), f32[256,512]{1,0:T(8,128)}) %reduce-scatter.31.cloned.1.call-update) | async-done | bytes 524304 | tf_op jit(solution)/shard_map/reduce_scatter | solution.py:284
  630.6 7.8 add_bitcast_fusion
  638.3 22.8 %reduce-scatter.39.cloned.1.call-done = f32[64,4]{1,0:T(8,128)} async-done(((f32[512,4]{1,0:T(8,128)}), f32[64,4]{1,0:T(8,128)}) %reduce-scatter.39.cloned.1.call-update) | async-done | bytes 1040
  662.0 9.8 %all-reduce = f32[4,64]{1,0:T(4,128)S(1)} all-reduce(f32[4,64]{1,0:T(4,128)S(1)} %copy.887), channel_id=13, replica_groups=mesh['batch'=4,'seq'=8] {'batch'}, use_global_device_ids=true, to_apply=%region_51.52.clone | all-reduce | flops 256 | bytes 2048
  672.5 13.6 %reduce-scatter.25.cloned.1.call-done = f32[16,512]{1,0:T(8,128)} async-done(((f32[64,512]{1,0:T(8,128)}), f32[16,512]{1,0:T(8,128)}) %reduce-scatter.25.cloned.1.call-update) | async-done | bytes 32784 | tf_op jit(solution)/shard_map/reduce_scatter | solution.py:293
  687.5 25.7 %reduce-scatter.21.cloned.1.call-done = f32[16,1536]{1,0:T(8,128)} async-done(((f32[64,1536]{1,0:T(8,128)}), f32[16,1536]{1,0:T(8,128)}) %reduce-scatter.21.cloned.1.call-update) | async-done | bytes 98320 | tf_op jit(solution)/shard_map/reduce_scatter | solution.py:292
  716.1 24.8 %reduce-scatter.29.cloned.1.call-done = f32[16,2048]{1,0:T(8,128)} async-done(((f32[64,2048]{1,0:T(8,128)}), f32[16,2048]{1,0:T(8,128)}) %reduce-scatter.29.cloned.1.call-update) | async-done | bytes 131088 | tf_op jit(solution)/shard_map/reduce_scatter | solution.py:294
  743.1 25.5 %reduce-scatter.33.cloned.1.call-done = f32[64,512]{1,0:T(8,128)} async-done(((f32[256,512]{1,0:T(8,128)}), f32[64,512]{1,0:T(8,128)}) %reduce-scatter.33.cloned.1.call-update) | async-done | bytes 131088 | tf_op jit(solution)/shard_map/reduce_scatter | solution.py:295
  771.7 5.5 copy.788
  777.2 39.3 %psum.7 = f32[]{:T(128)} all-reduce(f32[]{:T(128)S(6)} %add.484), channel_id=1, replica_groups=mesh['batch'=4,'seq'=8] {'batch','seq'}, use_global_device_ids=true, to_apply=%region_53.54 | all-reduce | flops 1 | bytes 8 | tf_op jit(solution)/shard_map/psum | solution.py:299
  (591 shorter events, 279.2 us)
Async XLA Ops:
  7.2 105.5 %all-gather.5.cloned.1.call-start = ((), (), s32[]{:S(2)}) async-start(), calls=%async_computation.11 | async-start | bytes 1622016 | tf_op jit(solution)/shard_map/all_gather | solution.py:85
  8.8 221.9 %all-gather.7.cloned.1.call-start = ((), (), s32[]{:S(2)}) async-start(), calls=%async_computation.12 | async-start | bytes 2162688 | tf_op jit(solution)/shard_map/all_gather | solution.py:87
  10.4 253.6 %all-gather.9.cloned.1.call-start = ((), (), s32[]{:S(2)}) async-start(), calls=%async_computation.13 | async-start | bytes 2162688 | tf_op jit(solution)/shard_map/all_gather | solution.py:88
  12.0 435.9 %reduce-scatter.37.cloned.1.call-start = ((), (), s32[]{:S(2)}) async-start(), calls=%async_computation.23 | async-start | bytes 294912 | tf_op jit(solution)/shard_map/reduce_scatter | solution.py:247
  59.1 49.9 %copy-start.148 = (f32[1,512]{1,0:T(1,128)}, f32[1,512]{1,0:T(1,128)S(1)}, u32[]{:S(2)}) copy-start(f32[1,512]{1,0:T(1,128)S(1)} %get-tuple-element.188) | copy-start | bytes 6148
  103.9 122.8 %copy-start = (bf16[1,2048,512]{1,2,0:T(8,128)(2,1)}, bf16[1,2048,512]{1,2,0:T(8,128)(2,1)S(1)}, u32[]{:S(2)}) copy-start(bf16[1,2048,512]{1,2,0:T(8,128)(2,1)S(1)} %copy.630) | copy-start | bytes 6291460
  156.4 64.6 %copy-start.30 = (bf16[128,512]{0,1:T(8,128)(2,1)}, bf16[128,512]{0,1:T(8,128)(2,1)S(1)}, u32[]{:S(2)}) copy-start(bf16[128,512]{0,1:T(8,128)(2,1)S(1)} %copy.638) | copy-start | bytes 393220
  158.6 58.1 %copy-start.28 = (bf16[4,128,8,64]{1,0,3,2:T(4,128)(2,1)}, bf16[4,128,8,64]{1,0,3,2:T(4,128)(2,1)S(1)}, u32[]{:S(2)}) copy-start(bf16[4,128,8,64]{1,0,3,2:T(4,128)(2,1)S(1)} %reshape.566) | copy-start | bytes 1572868
  160.8 50.6 %copy-start.26 = (bf16[4,128,8,64]{1,0,3,2:T(4,128)(2,1)}, bf16[4,128,8,64]{1,0,3,2:T(4,128)(2,1)S(1)}, u32[]{:S(2)}) copy-start(bf16[4,128,8,64]{1,0,3,2:T(4,128)(2,1)S(1)} %reshape.562) | copy-start | bytes 1572868
  228.6 70.0 %copy-start.138 = (f32[2048]{0:T(1024)}, f32[2048]{0:T(1024)S(1)}, u32[]{:S(2)}) copy-start(f32[2048]{0:T(1024)S(1)} %broadcast_multiply_fusion.2) | copy-start | bytes 24580
  230.6 68.0 %copy-start.146 = (f32[2048]{0:T(1024)}, f32[2048]{0:T(1024)S(1)}, u32[]{:S(2)}) copy-start(f32[2048]{0:T(1024)S(1)} %fusion.175) | copy-start | bytes 24580
  358.3 96.7 %reduce-scatter.35.cloned.1.call-start = ((), (), s32[]{:S(2)}) async-start(), calls=%async_computation.22 | async-start | bytes 294912 | tf_op jit(solution)/shard_map/reduce_scatter | solution.py:244
  427.5 87.3 %reduce-scatter.23.cloned.1.call-start = ((), (), s32[]{:S(2)}) async-start(), calls=%async_computation.16 | async-start | bytes 1179648 | tf_op jit(solution)/shard_map/reduce_scatter | solution.py:278
  435.1 93.5 %reduce-scatter.19.cloned.1.call-start = ((), (), s32[]{:S(2)}) async-start(), calls=%async_computation.14 | async-start | bytes 3538944 | tf_op jit(solution)/shard_map/reduce_scatter | solution.py:275
  465.5 114.5 %reduce-scatter.27.cloned.1.call-start = ((), (), s32[]{:S(2)}) async-start(), calls=%async_computation.18 | async-start | bytes 4718592 | tf_op jit(solution)/shard_map/reduce_scatter | solution.py:281
  477.3 153.3 %reduce-scatter.31.cloned.1.call-start = ((), (), s32[]{:S(2)}) async-start(), calls=%async_computation.20 | async-start | bytes 4718592 | tf_op jit(solution)/shard_map/reduce_scatter | solution.py:284
  488.4 172.8 %reduce-scatter.39.cloned.1.call-start = ((), (), s32[]{:S(2)}) async-start(), calls=%async_computation.24 | async-start | bytes 294912
  514.8 171.4 %reduce-scatter.25.cloned.1.call-start = ((), (), s32[]{:S(2)}) async-start(), calls=%async_computation.17 | async-start | bytes 163840 | tf_op jit(solution)/shard_map/reduce_scatter | solution.py:293
  515.5 197.8 %reduce-scatter.21.cloned.1.call-start = ((), (), s32[]{:S(2)}) async-start(), calls=%async_computation.15 | async-start | bytes 491520 | tf_op jit(solution)/shard_map/reduce_scatter | solution.py:292
  528.6 212.2 %reduce-scatter.29.cloned.1.call-start = ((), (), s32[]{:S(2)}) async-start(), calls=%async_computation.19 | async-start | bytes 655360 | tf_op jit(solution)/shard_map/reduce_scatter | solution.py:294
  580.1 188.5 %reduce-scatter.33.cloned.1.call-start = ((), (), s32[]{:S(2)}) async-start(), calls=%async_computation.21 | async-start | bytes 655360 | tf_op jit(solution)/shard_map/reduce_scatter | solution.py:295
  771.5 47.5 %copy-start.106 = (f32[16,1536]{1,0:T(8,128)S(1)}, f32[16,1536]{1,0:T(8,128)}, u32[]{:S(2)}) copy-start(f32[16,1536]{1,0:T(8,128)} %param.21) | copy-start | bytes 294916
  771.5 47.5 %copy-start.107 = (f32[16,1536]{1,0:T(8,128)S(1)}, f32[16,1536]{1,0:T(8,128)}, u32[]{:S(2)}) copy-start(f32[16,1536]{1,0:T(8,128)} %reduce-scatter.21.cloned.1.call-done) | copy-start | bytes 294916
  771.5 47.5 %copy-start.140 = (f32[16,1536]{1,0:T(8,128)S(1)}, f32[16,1536]{1,0:T(8,128)}, u32[]{:S(2)}) copy-start(f32[16,1536]{1,0:T(8,128)} %param.31) | copy-start | bytes 294916
  771.6 48.2 %copy-start.102 = (f32[16,2048]{1,0:T(8,128)S(1)}, f32[16,2048]{1,0:T(8,128)}, u32[]{:S(2)}) copy-start(f32[16,2048]{1,0:T(8,128)} %param.23) | copy-start | bytes 393220
  771.6 48.2 %copy-start.104 = (f32[16,2048]{1,0:T(8,128)S(1)}, f32[16,2048]{1,0:T(8,128)}, u32[]{:S(2)}) copy-start(f32[16,2048]{1,0:T(8,128)} %reduce-scatter.29.cloned.1.call-done) | copy-start | bytes 393220
  771.6 48.2 %copy-start.132 = (f32[16,2048]{1,0:T(8,128)S(1)}, f32[16,2048]{1,0:T(8,128)}, u32[]{:S(2)}) copy-start(f32[16,2048]{1,0:T(8,128)} %param.33) | copy-start | bytes 393220
  771.6 48.2 %copy-start.133 = (f32[16,2048]{1,0:T(8,128)S(1)}, f32[16,2048]{1,0:T(8,128)}, u32[]{:S(2)}) copy-start(f32[16,2048]{1,0:T(8,128)} %param.28) | copy-start | bytes 393220
  771.6 49.0 %copy-start.103 = (f32[64,512]{1,0:T(8,128)S(1)}, f32[64,512]{1,0:T(8,128)}, u32[]{:S(2)}) copy-start(f32[64,512]{1,0:T(8,128)} %param.24) | copy-start | bytes 393220
  771.6 49.0 %copy-start.105 = (f32[64,512]{1,0:T(8,128)S(1)}, f32[64,512]{1,0:T(8,128)}, u32[]{:S(2)}) copy-start(f32[64,512]{1,0:T(8,128)} %reduce-scatter.33.cloned.1.call-done) | copy-start | bytes 393220
  771.6 49.0 %copy-start.134 = (f32[64,512]{1,0:T(8,128)S(1)}, f32[64,512]{1,0:T(8,128)}, u32[]{:S(2)}) copy-start(f32[64,512]{1,0:T(8,128)} %param.34) | copy-start | bytes 393220
  771.6 49.0 %copy-start.135 = (f32[64,512]{1,0:T(8,128)S(1)}, f32[64,512]{1,0:T(8,128)}, u32[]{:S(2)}) copy-start(f32[64,512]{1,0:T(8,128)} %param.29) | copy-start | bytes 393220
  (155 other events, 918.7 us)
Sparse Core Ops, SparseCore 0:
  11.6 58.0 all-gather.4
  73.2 55.5 all-gather.6
  132.4 55.3 all-gather.8
  358.4 27.3 reduce-scatter.36
  427.6 27.3 reduce-scatter.34
  457.1 30.5 reduce-scatter.22
  490.0 38.5 reduce-scatter.18
  530.9 49.0 reduce-scatter.26
  582.3 48.1 reduce-scatter.30
  632.6 28.5 reduce-scatter.38
  664.2 21.9 reduce-scatter.24
  688.8 24.4 reduce-scatter.20
  716.1 24.7 reduce-scatter.28
  743.8 24.7 reduce-scatter.32
where the time goes:
time: 840 us; the launch traced here: 829 us
  waiting for transfers between devices  217 us (26%)
  local copies, waits for them, and re-layouts  207 us (25%)
  blocking collectives  164 us (20%)
  matrix products  157 us (19%)
  other arithmetic  60.6 us (7%)
  between operations  22.8 us (3%)
    reduce_scatter x1, waiting for transfers between devices, body(): lax.psum_scatter(regroup(up_grad, 0, groups, seq_count), 'seq', scatter_d...  50.1 us
    all_gather x1, blocking collectives, body(): lax.all_gather(norm_copy, ('batch', 'seq'), axis=1, tiled=True)  43.3 us
    all_gather x1, blocking collectives, body(): lax.all_gather(proj_copy, ('batch', 'seq'), axis=0, tiled=True)  41.9 us
    unnamed x358, local copies, waits for them, and re-layouts  40.3 us
    psum x1, blocking collectives, body(): grad_norm = jnp.sqrt(lax.psum(local_squares, ('batch', 'seq')))  39.3 us
    reduce_scatter x1, waiting for transfers between devices, body(): lax.psum_scatter(regroup(down_grad, 0, groups, seq_count), 'seq', scatter...  33.8 us
    reduce_scatter x1, waiting for transfers between devices, body(): lax.psum_scatter(sectioned[0], 'batch', scatter_dimension=0, tiled=True)  25.7 us
    reduce_scatter x1, waiting for transfers between devices, body(): lax.psum_scatter(sectioned[3], 'batch', scatter_dimension=0, tiled=True)  25.5 us
  transfers between devices with their start and end apart: 14, of which 9 were waited for; matrix products, arithmetic and copies ran while one was open for 37% of the time, Pallas kernels for 0%

commit v1 on v0

v1 whole, which is shorter than its diff:
```python
import functools
import jax
import jax.numpy as jnp
from jax import lax
from jax.experimental import pallas as pl
from jax.experimental.pallas import tpu as pltpu
from jax.sharding import PartitionSpec as P

HEADS = 8
HD = 64
SPAN = 128
STEP = 10
LN_EPS = 1e-05
NEG_FILL = -1e30
CLIP = 1.0
BETA = 0.5
ADAM_EPS = 1e-08
DECAY = 0.1
RATES = (0.02, 0.3, 0.02, 0.02, 0.5)
BF = jnp.bfloat16
F32 = jnp.float32
LANES = 128
VMEM_LIMIT = 56 * 1024 * 1024


def dot(a, b, dims=((1,), (0,))):
    return lax.dot_general(a, b, (dims, ((), ())), preferred_element_type=F32)


def dot_nt(a, b):
    return dot(a, b, ((1,), (1,)))


def normalize(x):
    inv = 1.0 / x.shape[-1]
    centred = x - jnp.sum(x, axis=-1, keepdims=True) * inv
    spread = jnp.sum(centred * centred, axis=-1, keepdims=True) * inv
    rstd = lax.rsqrt(spread + LN_EPS)
    return centred * rstd, rstd


def norm_back(grad, gain, xhat, rstd):
    inv = 1.0 / grad.shape[-1]
    e = grad * gain
    mean_e = jnp.sum(e, axis=-1, keepdims=True) * inv
    mean_ex = jnp.sum(e * xhat, axis=-1, keepdims=True) * inv
    return rstd * (e - mean_e - xhat * mean_ex)


def qkv_tile(x, norms_ref, weight_ref):
    xhat, _ = normalize(x.astype(F32))
    normed = (xhat * norms_ref[0:1, :] + norms_ref[1:2, :]).astype(BF)
    return dot(normed, weight_ref[...]).astype(BF)


def span_scale(length, begin, shape):
    count = jnp.clip(length - begin, 1, SPAN)
    return lax.rsqrt(jnp.full(shape, count, jnp.int32).astype(F32))


def span_sum(kv, length, begin):
    row = lax.broadcasted_iota(jnp.int32, kv.shape, 0)
    kept = jnp.where(row < length - begin, kv.astype(F32), 0.0)
    total = jnp.sum(kept, axis=0, keepdims=True)
    return total * span_scale(length, begin, total.shape)


def stack_heads(pair):
    lane = lax.broadcasted_iota(jnp.int32, pair.shape, 1)
    zero = jnp.zeros_like(pair)
    return jnp.concatenate(
        [jnp.where(lane < HD, pair, zero), jnp.where(lane >= HD, pair, zero)], axis=0
    )


def fold_heads(both):
    picked = jnp.concatenate([both[:HD, :SPAN], both[HD:, SPAN:]], axis=0)
    return picked.T


def masked_scores(keys, query2, near_cap, far_cap):
    raw = dot_nt(keys, query2)
    far = raw.shape[0] - SPAN
    key_pos = lax.broadcasted_iota(jnp.int32, (SPAN, 2 * SPAN), 0)
    near = jnp.where(key_pos <= near_cap, raw[:SPAN], NEG_FILL)
    summ_pos = lax.broadcasted_iota(jnp.int32, (far, 2 * SPAN), 0)
    far = jnp.where(summ_pos < far_cap, raw[SPAN:], NEG_FILL)
    return jnp.concatenate([near, far], axis=0)


def span_caps(length, span):
    query_pos = lax.broadcasted_iota(jnp.int32, (1, 2 * SPAN), 1) & (SPAN - 1)
    near_cap = jnp.minimum(query_pos, length - span * SPAN - 1)
    far_cap = jnp.minimum(span, (length + SPAN - 1) // SPAN)
    return near_cap, far_cap


def attend_span(mixed_ref, row, width, summ_ref, summ_vt_ref, caps, out_ref, out_row, lse_store):
    near_cap, far_cap = caps
    rows = pl.ds(row, SPAN)
    for pair in range(width // LANES):
        at = pair * LANES
        query2 = stack_heads(mixed_ref[rows, at : at + LANES] * BF(0.125))
        keys = jnp.concatenate(
            [mixed_ref[rows, width + at : width + at + LANES], summ_ref[:, at : at + LANES]], axis=0
        )
        values_t = jnp.concatenate(
            [
                mixed_ref[rows, 2 * width + at : 2 * width + at + LANES].T,
                summ_vt_ref[at : at + LANES, :],
            ],
            axis=1,
        )
        scores = masked_scores(keys, query2, near_cap, far_cap)
        peak = jnp.max(scores, axis=0, keepdims=True)
        expo = jnp.exp(scores - peak)
        total = jnp.sum(expo, axis=0, keepdims=True)
        out_t = dot(values_t, expo.astype(BF)) * (1.0 / total)
        out_ref[pl.ds(out_row, SPAN), at : at + LANES] = fold_heads(out_t).astype(BF)
        lse_store(pair, peak + jnp.log(total))


def attend_back_span(
    mixed_ref, grad_ref, row, width, summ_ref, summ_kt_ref, caps, lse_load, dq_ref, dkv_ref, out_row, dsumm_ref
):
    near_cap, far_cap = caps
    rows = pl.ds(row, SPAN)
    for pair in range(width // LANES):
        at = pair * LANES
        query2 = stack_heads(mixed_ref[rows, at : at + LANES] * BF(0.125))
        grad2 = stack_heads(grad_ref[rows, at : at + LANES])
        near_k = mixed_ref[rows, width + at : width + at + LANES]
        keys = jnp.concatenate([near_k, summ_ref[:, at : at + LANES]], axis=0)
        keys_t = jnp.concatenate([near_k.T, summ_kt_ref[at : at + LANES, :]], axis=1)
        values = jnp.concatenate(
            [
                mixed_ref[rows, 2 * width + at : 2 * width + at + LANES],
                summ_ref[:, width + at : width + at + LANES],
            ],
            axis=0,
        )
        scores = masked_scores(keys, query2, near_cap, far_cap)
        probs = jnp.exp(scores - lse_load(pair))
        dprob = dot_nt(values, grad2)
        delta = jnp.sum(probs * dprob, axis=0, keepdims=True)
        dscore = (probs * (dprob - delta)).astype(BF)
        dq = fold_heads(dot(keys_t, dscore)) * 0.125
        dk = dot(dscore, query2)
        dv = dot(probs.astype(BF), grad2)
        out = pl.ds(out_row, SPAN)
        dq_ref[out, at : at + LANES] = dq.astype(dq_ref.dtype)
        dkv_ref[out, at : at + LANES] = dk[:SPAN]
        dkv_ref[out, width + at : width + at + LANES] = dv[:SPAN]
        dsumm_ref[:, at : at + LANES] += dk[SPAN:]
        dsumm_ref[:, width + at : width + at + LANES] += dv[SPAN:]


GELU_A = 0.7978845608
GELU_B = 0.044715


def gelu_parts(t):
    sq = t * t
    th = jnp.tanh(t * (GELU_A + (GELU_A * GELU_B) * sq))
    half = 0.5 * th + 0.5
    slope = half + (2.0 * t) * (half * (1.0 - half)) * (GELU_A + (3.0 * GELU_A * GELU_B) * sq)
    return t * half, slope


def qkv_kernel(info_ref, x_ref, norms_ref, weight_ref, mixed_ref, summ_ref, sum_scr):
    step = pl.program_id(0)
    tile, width = x_ref.shape
    length, first_span = info_ref[0], info_ref[1]
    mixed = qkv_tile(x_ref[...], norms_ref, weight_ref)
    mixed_ref[...] = mixed
    per = tile // SPAN
    for part in range(per):
        span = step * per + part
        sum_scr[pl.ds(span, 1), :] = span_sum(
            mixed[part * SPAN : (part + 1) * SPAN, width:], length, (first_span + span) * SPAN
        )

    @pl.when(step == pl.num_programs(0) - 1)
    def _():
        summ_ref[...] = sum_scr[...].astype(BF)


def attend_kernel(info_ref, mixed_ref, summ_ref, out_ref, lse_ref, vt_scr):
    step = pl.program_id(0)
    width = out_ref.shape[1]

    @pl.when(step == 0)
    def _():
        vt_scr[...] = summ_ref[:, width:].T

    caps = span_caps(info_ref[0], info_ref[1] + step)

    def keep(pair, value):
        lse_ref[0, pair : pair + 1, :] = value

    attend_span(mixed_ref, 0, width, summ_ref, vt_scr, caps, out_ref, 0, keep)


def attend_back_kernel(info_ref, mixed_ref, grad_ref, lse_ref, summ_ref, dq_ref, dkv_ref, dsumm_ref, kt_scr):
    step = pl.program_id(0)
    width = dq_ref.shape[1]

    @pl.when(step == 0)
    def _():
        kt_scr[...] = summ_ref[:, :width].T
        dsumm_ref[...] = jnp.zeros_like(dsumm_ref)

    caps = span_caps(info_ref[0], info_ref[1] + step)
    attend_back_span(
        mixed_ref, grad_ref, 0, width, summ_ref, kt_scr, caps,
        lambda pair: lse_ref[0, pair : pair + 1, :], dq_ref, dkv_ref, 0, dsumm_ref,
    )


def mlp_kernel(
    x_ref, attn_ref, og_ref, norms_ref, proj_ref, up_ref, down_ref,
    out_ref, resid_grad_ref, attn_grad_ref, proj_grad_ref, up_grad_ref, down_grad_ref, norm_grad_ref,
    activ_scr, pre_grad_scr, n2t_scr, attnt_scr, ogt_scr, pig_scr, norm_scr,
):
    step = pl.program_id(0)
    tile, width = x_ref.shape
    hidden = up_ref.shape[1]
    rows = pl.ds(pl.multiple_of(step * tile, tile), tile)
    chunk = 512
    attn = attn_ref[...]
    grad = og_ref[...]
    resid = x_ref[...].astype(F32) + dot(attn, proj_ref[...])
    xhat, rstd = normalize(resid)
    gain = norms_ref[2:3, :]
    normed = (xhat * gain + norms_ref[3:4, :]).astype(BF)
    attnt_scr[:, rows] = attn.T
    n2t_scr[:, rows] = normed.T
    ogt_scr[:, rows] = grad.T
    acc = resid
    back = jnp.zeros_like(resid)
    for at in range(0, hidden, chunk):
        pre = dot(normed, up_ref[:, at : at + chunk])
        act_grad = dot_nt(grad, down_ref[at : at + chunk, :])
        value, slope = gelu_parts(pre)
        activ = value.astype(BF)
        pre_grad = (act_grad * slope).astype(BF)
        activ_scr[rows, at : at + chunk] = activ
        pre_grad_scr[rows, at : at + chunk] = pre_grad
        acc = acc + dot(activ, down_ref[at : at + chunk, :])
        back = back + dot_nt(pre_grad, up_ref[:, at : at + chunk])
    out_ref[...] = acc.astype(BF)
    resid_grad = grad.astype(F32) + norm_back(back, gain, xhat, rstd)
    resid_grad_ref[...] = resid_grad
    pig = resid_grad.astype(BF)
    pig_scr[rows, :] = pig
    attn_grad_ref[...] = dot_nt(pig, proj_ref[...]).astype(BF)
    gain_part = jnp.sum(back * xhat, axis=0, keepdims=True)
    shift_part = jnp.sum(back, axis=0, keepdims=True)
    part = jnp.concatenate([gain_part, shift_part], axis=0)

    @pl.when(step == 0)
    def _():
        norm_scr[...] = part

    @pl.when(step > 0)
    def _():
        norm_scr[...] += part

    @pl.when(step == pl.num_programs(0) - 1)
    def _():
        norm_grad_ref[...] = norm_scr[...]
        proj_grad_ref[...] = dot(attnt_scr[...], pig_scr[...])
        cols = 256

        def one(index, carry):
            c = pl.ds(pl.multiple_of(index * cols, cols), cols)
            up_grad_ref[:, c] = dot(n2t_scr[...], pre_grad_scr[:, c])
            down_grad_ref[c, :] = dot(ogt_scr[...], activ_scr[:, c]).T
            return carry

        lax.fori_loop(0, hidden // cols, one, 0)


def final_kernel(
    info_ref, x_ref, dq_ref, dkv_ref, extra_ref, resid_grad_ref, norms_ref, weight_ref,
    input_grad_ref, qkv_grad_ref, norm_grad_ref, mg_scr, n1t_scr, norm_scr,
):
    step = pl.program_id(0)
    tile, width = x_ref.shape
    rows = pl.ds(pl.multiple_of(step * tile, tile), tile)
    length, first_span = info_ref[0], info_ref[1]
    xhat, rstd = normalize(x_ref[...].astype(F32))
    gain = norms_ref[0:1, :]
    normed = (xhat * gain + norms_ref[1:2, :]).astype(BF)
    n1t_scr[:, rows] = normed.T
    per = tile // SPAN
    parts = []
    for part in range(per):
        span = step * per + part
        begin = (first_span + span) * SPAN
        extra = extra_ref[pl.ds(span, 1), :]
        extra = extra * span_scale(length, begin, extra.shape)
        local = dkv_ref[part * SPAN : (part + 1) * SPAN, :]
        pos = lax.broadcasted_iota(jnp.int32, local.shape, 0)
        parts.append(local + jnp.where(pos < length - begin, extra, 0.0))
    mg = jnp.concatenate([dq_ref[...], jnp.concatenate(parts, axis=0).astype(BF)], axis=1)
    mg_scr[rows, :] = mg
    back = dot_nt(mg, weight_ref[...])
    input_grad_ref[...] = resid_grad_ref[...] + norm_back(back, gain, xhat, rstd)
    gain_part = jnp.sum(back * xhat, axis=0, keepdims=True)
    shift_part = jnp.sum(back, axis=0, keepdims=True)
    part = jnp.concatenate([gain_part, shift_part], axis=0)

    @pl.when(step == 0)
    def _():
        norm_scr[...] = part

    @pl.when(step > 0)
    def _():
        norm_scr[...] += part

    @pl.when(step == pl.num_programs(0) - 1)
    def _():
        norm_grad_ref[...] = norm_scr[...]
        cols = 256

        def one(index, carry):
            c = pl.ds(pl.multiple_of(index * cols, cols), cols)
            qkv_grad_ref[:, c] = dot(n1t_scr[...], mg_scr[:, c])
            return carry

        lax.fori_loop(0, qkv_grad_ref.shape[1] // cols, one, 0)


def whole(shape):
    return pl.BlockSpec(shape, lambda i: (0,) * len(shape))


def by_rows(tile, width):
    return pl.BlockSpec((tile, width), lambda i: (i, 0))


SCALARS = pl.BlockSpec(memory_space=pltpu.SMEM)
PARAMS = pltpu.CompilerParams(vmem_limit_bytes=VMEM_LIMIT)


def regroup(grad, dim, outer, inner):
    shape = grad.shape
    piece = shape[dim] // (outer * inner)
    split = grad.reshape(shape[:dim] + (outer, inner, piece) + shape[dim + 1 :])
    return jnp.swapaxes(split, dim, dim + 1).reshape(shape)


def body(
    inputs, out_grad, lengths, qkv_weight, proj_weight, up_weight, down_weight, norm_params,
    qkv_mean, proj_mean, up_mean, down_mean, norm_mean,
    qkv_second, proj_second, up_second, down_second, norm_second,
):
    both = ("batch", "seq")
    gather = lambda w, axis: lax.all_gather(w.astype(BF), both, axis=axis, tiled=True)
    qkv_full = gather(qkv_weight, 0)
    proj_full = gather(proj_weight, 0)
    up_full = gather(up_weight, 0)
    down_full = gather(down_weight, 0)
    norms = gather(norm_params, 1).astype(F32)
    rows, width = inputs.shape[1], inputs.shape[2]
    hidden = up_full.shape[1]
    local = rows // SPAN
    spans = local * lax.axis_size("seq")
    first_span = lax.axis_index("seq") * local
    length = lengths[0]
    info = jnp.stack([length, first_span.astype(jnp.int32)])
    x, grad_rows = inputs[0], out_grad[0]
    tile = 256
    steps = rows // tile
    sds = jax.ShapeDtypeStruct
    mixed, own_summ = pl.pallas_call(
        qkv_kernel,
        grid=(steps,),
        in_specs=[SCALARS, by_rows(tile, width), whole(norms.shape), whole(qkv_full.shape)],
        out_specs=[by_rows(tile, 3 * width), whole((local, 2 * width))],
        out_shape=[sds((rows, 3 * width), BF), sds((local, 2 * width), BF)],
        scratch_shapes=[pltpu.VMEM((local, 2 * width), F32)],
        compiler_params=PARAMS,
        name="qkv",
    )(info, x, norms, qkv_full)
    summ = lax.all_gather(own_summ, "seq", axis=0, tiled=True)
    pairs = width // LANES
    lse_spec = pl.BlockSpec((1, pairs, 2 * SPAN), lambda i: (i, 0, 0))
    attn_out, lse = pl.pallas_call(
        attend_kernel,
        grid=(local,),
        in_specs=[SCALARS, by_rows(SPAN, 3 * width), whole(summ.shape)],
        out_specs=[by_rows(SPAN, width), lse_spec],
        out_shape=[sds((rows, width), BF), sds((local, pairs, 2 * SPAN), F32)],
        scratch_shapes=[pltpu.VMEM((width, spans), BF)],
        compiler_params=PARAMS,
        name="attend",
    )(info, mixed, summ)
    outputs, resid_grad, attn_grad, proj_grad, up_grad, down_grad, norm_two = pl.pallas_call(
        mlp_kernel,
        grid=(steps,),
        in_specs=[by_rows(tile, width)] * 3
        + [whole(norms.shape), whole(proj_full.shape), whole(up_full.shape), whole(down_full.shape)],
        out_specs=[by_rows(tile, width)] * 3
        + [whole(proj_full.shape), whole(up_full.shape), whole(down_full.shape), whole((2, width))],
        out_shape=[
            sds((rows, width), BF), sds((rows, width), F32), sds((rows, width), BF),
            sds(proj_full.shape, F32), sds(up_full.shape, F32), sds(down_full.shape, F32),
            sds((2, width), F32),
        ],
        scratch_shapes=[
            pltpu.VMEM((rows, hidden), BF), pltpu.VMEM((rows, hidden), BF),
            pltpu.VMEM((width, rows), BF), pltpu.VMEM((width, rows), BF), pltpu.VMEM((width, rows), BF),
            pltpu.VMEM((rows, width), BF), pltpu.VMEM((2, width), F32),
        ],
        compiler_params=PARAMS,
        name="mlp",
    )(x, attn_out, grad_rows, norms, proj_full, up_full, down_full)
    dq, dkv, dsumm = pl.pallas_call(
        attend_back_kernel,
        grid=(local,),
        in_specs=[SCALARS, by_rows(SPAN, 3 * width), by_rows(SPAN, width), lse_spec, whole(summ.shape)],
        out_specs=[by_rows(SPAN, width), by_rows(SPAN, 2 * width), whole((spans, 2 * width))],
        out_shape=[sds((rows, width), BF), sds((rows, 2 * width), F32), sds((spans, 2 * width), F32)],
        scratch_shapes=[pltpu.VMEM((width, spans), BF)],
        compiler_params=PARAMS,
        name="attend_back",
    )(info, mixed, attn_grad, lse, summ)
    extra = lax.psum_scatter(dsumm, "seq", scatter_dimension=0, tiled=True)
    input_grad, qkv_grad, norm_one = pl.pallas_call(
        final_kernel,
        grid=(steps,),
        in_specs=[
            SCALARS, by_rows(tile, width), by_rows(tile, width), by_rows(tile, 2 * width),
            whole(extra.shape), by_rows(tile, width), whole(norms.shape), whole(qkv_full.shape),
        ],
        out_specs=[by_rows(tile, width), whole(qkv_full.shape), whole((2, width))],
        out_shape=[sds((rows, width), F32), sds(qkv_full.shape, F32), sds((2, width), F32)],
        scratch_shapes=[
            pltpu.VMEM((rows, 3 * width), BF), pltpu.VMEM((width, rows), BF), pltpu.VMEM((2, width), F32),
        ],
        compiler_params=PARAMS,
        name="final",
    )(info, x, dq, dkv, extra, resid_grad, norms, qkv_full)
    norm_grad = jnp.concatenate([norm_one, norm_two], axis=0)
    groups = lax.axis_size("batch")
    seq_count = lax.axis_size("seq")
    reduced = []
    for grad, dim in ((qkv_grad, 0), (proj_grad, 0), (up_grad, 0), (down_grad, 0), (norm_grad, 1)):
        part = lax.psum_scatter(
            regroup(grad, dim, groups, seq_count), "seq", scatter_dimension=dim, tiled=True
        )
        reduced.append(lax.psum_scatter(part, "batch", scatter_dimension=dim, tiled=True))
    local_squares = sum((jnp.sum(grad * grad) for grad in reduced))
    grad_norm = jnp.sqrt(lax.psum(local_squares, both))
    factor = jnp.minimum(1.0, CLIP / (grad_norm + 1e-06))
    fix = 1.0 - BETA**STEP
    masters = (qkv_weight, proj_weight, up_weight, down_weight, norm_params)
    firsts = (qkv_mean, proj_mean, up_mean, down_mean, norm_mean)
    seconds = (qkv_second, proj_second, up_second, down_second, norm_second)
    moments, squares, fresh = ([], [], [])
    for grad, master, first, second, rate in zip(reduced, masters, firsts, seconds, RATES):
        clipped = grad * factor
        moment = BETA * first + (1.0 - BETA) * clipped
        square = BETA * second + (1.0 - BETA) * clipped * clipped
        update = moment / fix / (jnp.sqrt(square / fix) + ADAM_EPS)
        moments.append(moment)
        squares.append(square)
        fresh.append(master - rate * (update + DECAY * master))
    shift_clipped = reduced[4][3] * factor
    return (
        outputs[None], input_grad[None], grad_norm, *moments, *squares, *fresh, shift_clipped,
    )


def solution(mesh):
    tokens = P("batch", "seq", None)
    owned = P(("batch", "seq"), None)
    columns = P(None, ("batch", "seq"))
    state = (owned, owned, owned, owned, columns)
    return jax.shard_map(
        body,
        mesh=mesh,
        in_specs=(tokens, tokens, P("batch")) + state * 3,
        out_specs=(tokens, tokens, P()) + state * 3 + (P(("batch", "seq")),),
        check_vma=False,
    )
```

time: 840 us -> 670 us (0.80); the launches traced: 829 us -> 668 us
  local copies, waits for them, and re-layouts: 207 us -> 18.5 us
  matrix products: 157 us -> 0 us
  Pallas kernels: 0 us -> 131 us
  waiting for transfers between devices: 217 us -> 326 us
  other arithmetic: 60.6 us -> 20.9 us
  blocking collectives: 164 us -> 151 us
    dot_general x62 -> x0, matrix products: 157 us -> none  [the longest x1 16.5 us: body(): jnp.einsum('td,fd->tf', grad_rows, down_back, preferred_element_type=jnp....]
    pallas_call x0 -> x5, Pallas kernels: none -> 131 us  [the longest x1 49.7 us: body(): pl.pallas_call(mlp_kernel, grid=(steps,), in_specs=[by_rows(tile, width)]...]
    reshape x48 -> x1, local copies, waits for them, and re-layouts: 109 us -> 0.09 us  [regroup(): split = grad.reshape(shape[:dim] + (outer, inner, piece) + shape[dim + 1:])]
    reduce_scatter x10 -> x9, waiting for transfers between devices: 194 us -> 259 us  [the longest x4 141 us: body(): lax.psum_scatter(regroup(grad, dim, groups, seq_count), 'seq', scatter_di...]
    unnamed x358 -> x41, local copies, waits for them, and re-layouts: 40.3 us -> 2.96 us
    all_gather x3, waiting for transfers between devices: 0.01 us -> 35.9 us  [body(): lax.all_gather(w.astype(BF), both, axis=axis, tiled=True)]
    dot_general x3 -> x0, local copies, waits for them, and re-layouts: 29 us -> none  [the longest x1 17.8 us: body(): pre_act = jnp.dot(normed_two, up_full, preferred_element_type=jnp.float32)]
    slice x12 -> x0, local copies, waits for them, and re-layouts: 17.5 us -> none  [the longest x5 8.74 us: block_pieces(): query[begin:ending].reshape(shape)]
  transfers between devices with their start and end apart: 14 -> 13, of which waited for: 9 -> 10; matrix products, arithmetic and copies ran while one was open for 37% -> 4% of each run, Pallas kernels for 0% -> 8%
where the time goes in v1:
time: 670 us; the launch traced here: 668 us
  waiting for transfers between devices  326 us (49%)
  blocking collectives  151 us (23%)
  Pallas kernels  131 us (20%)
  other arithmetic  20.9 us (3%)
  between operations  20.6 us (3%)
  local copies, waits for them, and re-layouts  18.5 us (3%)
    reduce_scatter x4, waiting for transfers between devices, body(): lax.psum_scatter(regroup(grad, dim, groups, seq_count), 'seq', scatter_di...  141 us
    reduce_scatter x4, waiting for transfers between devices, body(): lax.psum_scatter(part, 'batch', scatter_dimension=dim, tiled=True)  89.7 us
    all_gather x2, blocking collectives, body(): lax.all_gather(w.astype(BF), both, axis=axis, tiled=True)  85.4 us
    pallas_call x1, Pallas kernels, body(): pl.pallas_call(mlp_kernel, grid=(steps,), in_specs=[by_rows(tile, width)]...  49.7 us
    psum x1, blocking collectives, body(): grad_norm = jnp.sqrt(lax.psum(local_squares, both))  39.3 us
    all_gather x3, waiting for transfers between devices, body(): lax.all_gather(w.astype(BF), both, axis=axis, tiled=True)  35.9 us
    unnamed x14, waiting for transfers between devices  30.3 us
    reduce_scatter x1, waiting for transfers between devices, body(): extra = lax.psum_scatter(dsumm, 'seq', scatter_dimension=0, tiled=True)  28.8 us
  transfers between devices with their start and end apart: 13, of which 10 were waited for; matrix products, arithmetic and copies ran while one was open for 4% of the time, Pallas kernels for 8%

profile of v1, /device:TPU:0, one launch (start us, length us, event | category | flops | bytes accessed | tf_op | source)
XLA Modules:
  0.0 668.2 jit_solution(14912205092611840747)
XLA Ops:
  7.2 1.5 convert_element_type.20
  8.8 1.5 convert_element_type.22
  10.4 1.5 convert_element_type.23
  14.2 43.3 %all-gather = bf16[32,16,4]{1,2,0:T(4,128)(2,1)S(1)} all-gather(bf16[1,16,4]{1,2,0:T(4,128)(2,1)S(1)} %convert_bitcast_fusion), channel_id=1, replica_groups=mesh['batch'=4,'seq'=8] {'batch','seq'}, dimensions={0}, use_global_device_ids=true | all-gather | bytes 4224 | tf_op jit(solution)/shard_map/all_gather | solution.py:360
  58.9 42.2 %all_gather.21.proj_ref = bf16[512,512]{1,0:T(8,128)(2,1)} all-gather(bf16[16,512]{1,0:T(8,128)(2,1)S(1)} %convert_element_type.21), channel_id=1, replica_groups=mesh['batch'=4,'seq'=8] {'batch','seq'}, dimensions={0}, use_global_device_ids=true | all-gather | bytes 540672 | tf_op jit(solution)/shard_map/all_gather | solution.py:360
  101.1 10.2 %qkv.1 = (bf16[2048,1536]{1,0:T(8,128)(2,1)}, bf16[16,1024]{1,0:T(8,128)(2,1)}) custom-call(s32[2]{0:T(128)} %pad_add_fusion.info_ref, bf16[2048,512]{1,0:T(8,128)(2,1)} %bitcast.38, f32[4,512]{1,0:T(4,128)} %bitcast.52, bf16[512,1536]{1,0:T(8,128)(2,1)} %all-gather.5.cloned.1.call-done.weight_ref), custom_call_target="tpu_custom_call" | custom-call | tf_op jit(solution)/shard_map/qkv/pallas_call | solution.py:377
  111.3 16.1 %all_gather.20.summ_ref = bf16[128,1024]{1,0:T(8,128)(2,1)} all-gather(bf16[16,1024]{1,0:T(8,128)(2,1)} %get-tuple-element.37), channel_id=1, replica_groups=mesh['batch'=4,'seq'=8] {'seq'}, dimensions={0}, use_global_device_ids=true | all-gather | bytes 294912 | tf_op jit(solution)/shard_map/all_gather | solution.py:387
  127.4 24.3 %attend.1 = (bf16[2048,512]{1,0:T(8,128)(2,1)}, f32[16,4,256]{2,1,0:T(4,128)}) custom-call(s32[2]{0:T(128)} %pad_add_fusion.info_ref, bf16[2048,1536]{1,0:T(8,128)(2,1)} %get-tuple-element.36.mixed_ref, bf16[128,1024]{1,0:T(8,128)(2,1)} %all_gather.20.summ_ref), custom_call_target="tpu_custom_call" | custom-call | tf_op jit(solution)/shard_map/attend/pallas_call | solution.py:390
  151.7 35.9 %all-gather.9.cloned.1.call-done.down_ref = bf16[2048,512]{1,0:T(8,128)(2,1)} async-done(((bf16[64,512]{1,0:T(8,128)(2,1)}), bf16[2048,512]{1,0:T(8,128)(2,1)}) %all-gather.9.cloned.1.call-update) | async-done | bytes 2097168 | tf_op jit(solution)/shard_map/all_gather | solution.py:360
  187.7 49.7 %mlp.1 = (bf16[2048,512]{1,0:T(8,128)(2,1)}, f32[2048,512]{1,0:T(8,128)}, bf16[2048,512]{1,0:T(8,128)(2,1)}, f32[512,512]{1,0:T(8,128)}, f32[512,2048]{1,0:T(8,1...) custom-call(bf16[2048,512]{1,0:T(8,128)(2,1)} %bitcast.39, bf16[2048,512]{1,0:T(8,128)(2,1)} %get-tuple-element.38.attn_ref, ...), custom_call_target="tpu_custom_call" | custom-call | tf_op jit(solution)/shard_map/mlp/pallas_call | solution.py:400
  237.4 28.6 %attend_back.1 = (bf16[2048,512]{1,0:T(8,128)(2,1)}, f32[2048,1024]{1,0:T(8,128)}, f32[128,1024]{1,0:T(8,128)}) custom-call(s32[2]{0:T(128)} %pad_add_fusion.info_ref, bf16[2048,1536]{1,0:T(8,128)(2,1)} %get-tuple-element.36.mixed_ref, bf16[2048,512]{1,0:T(8,128)(2,1)} %get-tuple-element.40.grad_ref, f32[16,4,256]{2,1,0:T(4,128)} %get-tuple-element.41.lse_ref, ...), custom_call_target="tpu_custom_call" | custom-call | tf_op jit(solution)/shard_map/attend_back/pallas_call | solution.py:420
  267.2 28.8 %reduce-scatter.14.cloned.1.call-done.extra_ref = f32[16,1024]{1,0:T(8,128)} async-done(((f32[128,1024]{1,0:T(8,128)}), f32[16,1024]{1,0:T(8,128)}) %reduce-scatter.14.cloned.1.call-update) | async-done | bytes 65552 | tf_op jit(solution)/shard_map/reduce_scatter | solution.py:430
  296.0 18.3 %final.1 = (f32[2048,512]{1,0:T(8,128)}, f32[512,1536]{1,0:T(8,128)}, f32[2,512]{1,0:T(2,128)}) custom-call(s32[2]{0:T(128)} %pad_add_fusion.info_ref, bf16[2048,512]{1,0:T(8,128)(2,1)} %bitcast.40, bf16[2048,512]{1,0:T(8,128)(2,1)} %get-tuple-element.42.dq_ref, f32[2048,1024]{1,0:T(8,128)} %get-tuple-element.43.dkv_ref, ...), custom_call_target="tpu_custom_call" | custom-call | tf_op jit(solution)/shard_map/final/pallas_call | solution.py:431
  314.3 4.0 copy.57
  318.5 4.6 copy.59
  323.2 4.9 copy.60
  330.6 39.0 %reduce-scatter.16.cloned.1.call-done = f32[64,1536]{1,0:T(8,128)} async-done(((f32[512,1536]{1,0:T(8,128)}), f32[64,1536]{1,0:T(8,128)}) %reduce-scatter.16.cloned.1.call-update) | async-done | bytes 393232 | tf_op jit(solution)/shard_map/reduce_scatter | solution.py:451
  369.6 51.5 %reduce-scatter.24.cloned.1.call-done = f32[64,2048]{1,0:T(8,128)} async-done(((f32[512,2048]{1,0:T(8,128)}), f32[64,2048]{1,0:T(8,128)}) %reduce-scatter.24.cloned.1.call-update) | async-done | bytes 524304 | tf_op jit(solution)/shard_map/reduce_scatter | solution.py:451
  421.2 50.5 %reduce-scatter.28.cloned.1.call-done = f32[256,512]{1,0:T(8,128)} async-done(((f32[2048,512]{1,0:T(8,128)}), f32[256,512]{1,0:T(8,128)}) %reduce-scatter.28.cloned.1.call-update) | async-done | bytes 524304 | tf_op jit(solution)/shard_map/reduce_scatter | solution.py:451
  473.0 29.6 %reduce-scatter.32.cloned.1.call-done = f32[64,4]{1,0:T(8,128)} async-done(((f32[512,4]{1,0:T(8,128)}), f32[64,4]{1,0:T(8,128)}) %reduce-scatter.32.cloned.1.call-update) | async-done | bytes 1040
  503.4 9.8 %all-reduce = f32[4,64]{1,0:T(4,128)S(1)} all-reduce(f32[4,64]{1,0:T(4,128)S(1)} %copy.63), channel_id=12, replica_groups=mesh['batch'=4,'seq'=8] {'batch'}, use_global_device_ids=true, to_apply=%region_14.0.clone | all-reduce | flops 256 | bytes 2048
  513.9 13.3 %reduce-scatter.22.cloned.1.call-done = f32[16,512]{1,0:T(8,128)} async-done(((f32[64,512]{1,0:T(8,128)}), f32[16,512]{1,0:T(8,128)}) %reduce-scatter.22.cloned.1.call-update) | async-done | bytes 32784 | tf_op jit(solution)/shard_map/reduce_scatter | solution.py:454
  528.5 26.1 %reduce-scatter.18.cloned.1.call-done = f32[16,1536]{1,0:T(8,128)} async-done(((f32[64,1536]{1,0:T(8,128)}), f32[16,1536]{1,0:T(8,128)}) %reduce-scatter.18.cloned.1.call-update) | async-done | bytes 98320 | tf_op jit(solution)/shard_map/reduce_scatter | solution.py:454
  554.6 1.5 multiply_reduce_fusion.2
  557.4 24.9 %reduce-scatter.26.cloned.1.call-done = f32[16,2048]{1,0:T(8,128)} async-done(((f32[64,2048]{1,0:T(8,128)}), f32[16,2048]{1,0:T(8,128)}) %reduce-scatter.26.cloned.1.call-update) | async-done | bytes 131088 | tf_op jit(solution)/shard_map/reduce_scatter | solution.py:454
  582.3 1.5 multiply_reduce_fusion.1
  584.5 25.4 %reduce-scatter.30.cloned.1.call-done = f32[64,512]{1,0:T(8,128)} async-done(((f32[256,512]{1,0:T(8,128)}), f32[64,512]{1,0:T(8,128)}) %reduce-scatter.30.cloned.1.call-update) | async-done | bytes 131088 | tf_op jit(solution)/shard_map/reduce_scatter | solution.py:454
  610.0 1.5 multiply_reduce_fusion
  612.8 39.3 %psum.7 = f32[]{:T(128)} all-reduce(f32[]{:T(128)S(6)} %add.117), channel_id=1, replica_groups=mesh['batch'=4,'seq'=8] {'batch','seq'}, use_global_device_ids=true, to_apply=%region_16.0 | all-reduce | flops 1 | bytes 8 | tf_op jit(solution)/shard_map/psum | solution.py:456
  655.4 1.6 multiply_subtract_fusion.2
  657.1 1.7 multiply_subtract_fusion.1
  658.8 1.7 multiply_subtract_fusion
  (84 shorter events, 13.0 us)
Async XLA Ops:
  7.2 93.9 %all-gather.5.cloned.1.call-start = ((), (), s32[]{:S(2)}) async-start(), calls=%async_computation.10 | async-start | bytes 1622016 | tf_op jit(solution)/shard_map/all_gather | solution.py:360
  8.8 143.0 %all-gather.7.cloned.1.call-start = ((), (), s32[]{:S(2)}) async-start(), calls=%async_computation.11 | async-start | bytes 2162688 | tf_op jit(solution)/shard_map/all_gather | solution.py:360
  10.4 177.3 %all-gather.9.cloned.1.call-start = ((), (), s32[]{:S(2)}) async-start(), calls=%async_computation.12 | async-start | bytes 2162688 | tf_op jit(solution)/shard_map/all_gather | solution.py:360
  12.0 284.0 %reduce-scatter.14.cloned.1.call-start = ((), (), s32[]{:S(2)}) async-start(), calls=%async_computation.13 | async-start | bytes 589824 | tf_op jit(solution)/shard_map/reduce_scatter | solution.py:430
  237.4 28.7 %copy-start = (f32[512,512]{1,0:T(8,128)S(1)}, f32[512,512]{1,0:T(8,128)}, u32[]{:S(2)}) copy-start(f32[512,512]{1,0:T(8,128)} %get-tuple-element.48) | copy-start | bytes 3145732
  266.0 64.0 %reduce-scatter.20.cloned.1.call-start = ((), (), s32[]{:S(2)}) async-start(), calls=%async_computation.16 | async-start | bytes 1179648 | tf_op jit(solution)/shard_map/reduce_scatter | solution.py:451
  267.2 102.4 %reduce-scatter.16.cloned.1.call-start = ((), (), s32[]{:S(2)}) async-start(), calls=%async_computation.14 | async-start | bytes 3538944 | tf_op jit(solution)/shard_map/reduce_scatter | solution.py:451
  318.3 102.8 %reduce-scatter.24.cloned.1.call-start = ((), (), s32[]{:S(2)}) async-start(), calls=%async_computation.18 | async-start | bytes 4718592 | tf_op jit(solution)/shard_map/reduce_scatter | solution.py:451
  323.2 148.5 %reduce-scatter.28.cloned.1.call-start = ((), (), s32[]{:S(2)}) async-start(), calls=%async_computation.20 | async-start | bytes 4718592 | tf_op jit(solution)/shard_map/reduce_scatter | solution.py:451
  328.1 0.7 copy-start.14
  328.1 0.7 copy-start.15
  328.1 143.6 %copy-start.18 = (u32[32]{0:T(128)S(1)}, u32[32]{0:T(128)}, u32[]{:S(2)}) copy-start(u32[32]{0:T(128)} %constant.69) | copy-start | bytes 388
  328.1 325.3 %copy-start.13 = (f32[4,16]{1,0:T(4,128)S(1)}, f32[4,16]{1,0:T(4,128)}, u32[]{:S(2)}) copy-start(f32[4,16]{1,0:T(4,128)} %param.25) | copy-start | bytes 772
  328.1 325.3 %copy-start.16 = (f32[4,16]{1,0:T(4,128)S(1)}, f32[4,16]{1,0:T(4,128)}, u32[]{:S(2)}) copy-start(f32[4,16]{1,0:T(4,128)} %param.35) | copy-start | bytes 772
  328.1 325.3 %copy-start.17 = (f32[4,16]{1,0:T(4,128)S(1)}, f32[4,16]{1,0:T(4,128)}, u32[]{:S(2)}) copy-start(f32[4,16]{1,0:T(4,128)} %param.30) | copy-start | bytes 772
  328.1 325.9 %copy-start.8 = (f32[16,512]{1,0:T(8,128)S(1)}, f32[16,512]{1,0:T(8,128)}, u32[]{:S(2)}) copy-start(f32[16,512]{1,0:T(8,128)} %param.22) | copy-start | bytes 98308
  328.2 325.9 %copy-start.11 = (f32[16,512]{1,0:T(8,128)S(1)}, f32[16,512]{1,0:T(8,128)}, u32[]{:S(2)}) copy-start(f32[16,512]{1,0:T(8,128)} %param.32) | copy-start | bytes 98308
  328.2 325.9 %copy-start.12 = (f32[16,512]{1,0:T(8,128)S(1)}, f32[16,512]{1,0:T(8,128)}, u32[]{:S(2)}) copy-start(f32[16,512]{1,0:T(8,128)} %param.27) | copy-start | bytes 98308
  328.2 327.3 %copy-start.3 = (f32[16,1536]{1,0:T(8,128)S(1)}, f32[16,1536]{1,0:T(8,128)}, u32[]{:S(2)}) copy-start(f32[16,1536]{1,0:T(8,128)} %param.21) | copy-start | bytes 294916
  328.2 327.2 %copy-start.9 = (f32[16,1536]{1,0:T(8,128)S(1)}, f32[16,1536]{1,0:T(8,128)}, u32[]{:S(2)}) copy-start(f32[16,1536]{1,0:T(8,128)} %param.31) | copy-start | bytes 294916
  328.2 327.2 %copy-start.10 = (f32[16,1536]{1,0:T(8,128)S(1)}, f32[16,1536]{1,0:T(8,128)}, u32[]{:S(2)}) copy-start(f32[16,1536]{1,0:T(8,128)} %param.26) | copy-start | bytes 294916
  328.2 328.9 %copy-start.1 = (f32[16,2048]{1,0:T(8,128)S(1)}, f32[16,2048]{1,0:T(8,128)}, u32[]{:S(2)}) copy-start(f32[16,2048]{1,0:T(8,128)} %param.23) | copy-start | bytes 393220
  328.2 328.9 %copy-start.4 = (f32[16,2048]{1,0:T(8,128)S(1)}, f32[16,2048]{1,0:T(8,128)}, u32[]{:S(2)}) copy-start(f32[16,2048]{1,0:T(8,128)} %param.33) | copy-start | bytes 393220
  328.2 328.9 %copy-start.5 = (f32[16,2048]{1,0:T(8,128)S(1)}, f32[16,2048]{1,0:T(8,128)}, u32[]{:S(2)}) copy-start(f32[16,2048]{1,0:T(8,128)} %param.28) | copy-start | bytes 393220
  328.3 330.5 %copy-start.2 = (f32[64,512]{1,0:T(8,128)S(1)}, f32[64,512]{1,0:T(8,128)}, u32[]{:S(2)}) copy-start(f32[64,512]{1,0:T(8,128)} %param.24) | copy-start | bytes 393220
  328.3 330.5 %copy-start.6 = (f32[64,512]{1,0:T(8,128)S(1)}, f32[64,512]{1,0:T(8,128)}, u32[]{:S(2)}) copy-start(f32[64,512]{1,0:T(8,128)} %param.34) | copy-start | bytes 393220
  328.3 330.5 %copy-start.7 = (f32[64,512]{1,0:T(8,128)S(1)}, f32[64,512]{1,0:T(8,128)}, u32[]{:S(2)}) copy-start(f32[64,512]{1,0:T(8,128)} %param.29) | copy-start | bytes 393220
  328.3 174.3 %reduce-scatter.32.cloned.1.call-start = ((), (), s32[]{:S(2)}) async-start(), calls=%async_computation.22 | async-start | bytes 294912
  329.9 197.2 %reduce-scatter.22.cloned.1.call-start = ((), (), s32[]{:S(2)}) async-start(), calls=%async_computation.17 | async-start | bytes 163840 | tf_op jit(solution)/shard_map/reduce_scatter | solution.py:454
  330.5 224.1 %reduce-scatter.18.cloned.1.call-start = ((), (), s32[]{:S(2)}) async-start(), calls=%async_computation.15 | async-start | bytes 491520 | tf_op jit(solution)/shard_map/reduce_scatter | solution.py:454
  369.6 212.8 %reduce-scatter.26.cloned.1.call-start = ((), (), s32[]{:S(2)}) async-start(), calls=%async_computation.19 | async-start | bytes 655360 | tf_op jit(solution)/shard_map/reduce_scatter | solution.py:454
  421.1 188.9 %reduce-scatter.30.cloned.1.call-start = ((), (), s32[]{:S(2)}) async-start(), calls=%async_computation.21 | async-start | bytes 655360 | tf_op jit(solution)/shard_map/reduce_scatter | solution.py:454
Sparse Core Ops, SparseCore 0:
  11.6 57.9 all-gather.4
  73.2 55.3 all-gather.6
  132.2 55.4 all-gather.8
  266.1 29.8 reduce-scatter.13
  298.2 30.4 reduce-scatter.19
  331.0 38.5 reduce-scatter.15
  371.9 49.0 reduce-scatter.23
  423.5 48.1 reduce-scatter.27
  474.0 28.5 reduce-scatter.31
  505.2 21.9 reduce-scatter.21
  530.2 24.4 reduce-scatter.17
  557.5 24.7 reduce-scatter.25
  585.2 24.7 reduce-scatter.29

commit v2 on v1

--- a/solution.py
+++ b/solution.py
@@ -167,6 +167,305 @@
     return t * half, slope
 
 
+MESH = pl.DeviceIdType.MESH
+
+
+class Place:
+    def __init__(self, groups, seqs):
+        self.groups, self.chips = groups, seqs // 2
+        self.b = lax.axis_index("batch")
+        seq = lax.axis_index("seq")
+        self.z, self.c = seq // 2, seq % 2
+        self.other = 1 - self.c
+        self.b1 = self.b + 1 - 2 * (self.b % 2)
+        self.b2 = (self.b + 2) % 4
+        self.b3 = self.b1 + 2 - 4 * (self.b1 // 2)
+
+    def at(self, b, z, c):
+        return (b, 2 * z + c)
+
+    def sibling(self):
+        return self.at(self.b, self.z, self.other)
+
+    def along(self, step):
+        return (self.z + step) % self.chips
+
+
+def meet(place):
+    barrier = pltpu.get_barrier_semaphore()
+    partners = [place.sibling(), place.at(place.b1, place.z, place.c), place.at(place.b2, place.z, place.c)]
+    partners += [place.at(place.b, place.along(k), place.c) for k in range(1, place.chips)]
+    for partner in partners:
+        pl.semaphore_signal(barrier, inc=1, device_id=partner, device_id_type=MESH)
+    pl.semaphore_wait(barrier, len(partners))
+
+
+class Copies:
+    def __init__(self, send_sems, recv_sems):
+        self.send, self.recv, self.made = send_sems, recv_sems, []
+
+    def start(self, src, dst, device):
+        at = len(self.made)
+        assert at < self.send.shape[0]
+        copy = pltpu.make_async_remote_copy(
+            src_ref=src, dst_ref=dst, send_sem=self.send.at[at], recv_sem=self.recv.at[at],
+            device_id=device, device_id_type=MESH,
+        )
+        copy.start()
+        self.made.append(copy)
+        return copy
+
+    def finish(self):
+        for copy in self.made:
+            copy.wait_send()
+
+
+def gather_steps(place, copies, full):
+    p, half = place, place.chips // 2
+    low, high = pl.ds(0, half), pl.ds(half, place.chips - half)
+    own = full.at[p.b, p.z, p.c]
+    along = [copies.start(own, own, p.at(p.b, p.along(k), p.c)) for k in range(1, p.chips)]
+    yield
+    for copy in along:
+        copy.wait_recv()
+    column = full.at[p.b, :, p.c]
+    to_x = copies.start(column, column, p.at(p.b1, p.z, p.c))
+    to_y = copies.start(column, column, p.at(p.b2, p.z, p.c))
+    sib = [copies.start(column, column, p.sibling())]
+    yield
+    to_x.wait_recv()
+    block = full.at[p.b1, low, p.c]
+    on_y = copies.start(block, block, p.at(p.b2, p.z, p.c))
+    to_y.wait_recv()
+    block = full.at[p.b2, high, p.c]
+    on_x = copies.start(block, block, p.at(p.b1, p.z, p.c))
+    for b in (p.b1, p.b2):
+        column = full.at[b, :, p.c]
+        sib.append(copies.start(column, column, p.sibling()))
+    yield
+    for copy, part in ((on_y, low), (on_x, high)):
+        copy.wait_recv()
+        block = full.at[p.b3, part, p.c]
+        sib.append(copies.start(block, block, p.sibling()))
+    yield
+    for copy in sib:
+        copy.wait_recv()
+
+
+GATHER_COPIES = 12
+
+
+def add_into(acc, index, other, part=None):
+    acc[index] = (acc[index].astype(F32) + other.astype(F32)).astype(acc.dtype)
+
+
+def scatter_steps(place, copies, grad, acc, got, near, far, last, result):
+    p, half = place, place.chips // 2
+    low, high = pl.ds(0, half), pl.ds(half, place.chips - half)
+    groups, chips = p.groups, p.chips
+    swap = copies.start(grad.at[:, :, p.other], got, p.sibling())
+    yield
+    swap.wait_recv()
+
+    def add_one(i, carry):
+        b, z = i // chips, i % chips
+        acc[b, z] = (grad[b, z, p.c].astype(F32) + got[b, z].astype(F32)).astype(BF)
+        return carry
+
+    lax.fori_loop(0, groups * chips, add_one, 0)
+    on_y = copies.start(acc.at[p.b3, low], far.at[0], p.at(p.b2, p.z, p.c))
+    on_x = copies.start(acc.at[p.b3, high], far.at[1], p.at(p.b1, p.z, p.c))
+    early_x = copies.start(acc.at[p.b1, high], near.at[0, high], p.at(p.b1, p.z, p.c))
+    early_y = copies.start(acc.at[p.b2, low], near.at[1, low], p.at(p.b2, p.z, p.c))
+    yield
+    on_y.wait_recv()
+    for z in range(half):
+        acc[p.b1, z] = (acc[p.b1, z].astype(F32) + far[0, z].astype(F32)).astype(BF)
+    late_x = copies.start(acc.at[p.b1, low], near.at[0, low], p.at(p.b1, p.z, p.c))
+    on_x.wait_recv()
+    for z in range(half, chips):
+        acc[p.b2, z] = (acc[p.b2, z].astype(F32) + far[1, z - half].astype(F32)).astype(BF)
+    late_y = copies.start(acc.at[p.b2, high], near.at[1, high], p.at(p.b2, p.z, p.c))
+    yield
+    for copy in (early_x, early_y, late_x, late_y):
+        copy.wait_recv()
+    for z in range(chips):
+        acc[p.b, z] = (acc[p.b, z].astype(F32) + near[0, z].astype(F32) + near[1, z].astype(F32)).astype(BF)
+    along = []
+    for k in range(1, chips):
+        to = p.along(k)
+        along.append(copies.start(acc.at[p.b, to], last.at[k - 1], p.at(p.b, to, p.c)))
+    yield
+    total = acc[p.b, p.z].astype(F32)
+    for k, copy in enumerate(along):
+        copy.wait_recv()
+        total = total + last[k].astype(F32)
+    result[...] = total
+
+
+SCATTER_COPIES = 10
+
+
+def scatter_scratch(groups, chips, rows, cols):
+    half = chips // 2
+    return [
+        pltpu.VMEM((groups, chips, rows, cols), BF),
+        pltpu.VMEM((groups, chips, rows, cols), BF),
+        pltpu.VMEM((2, chips, rows, cols), BF),
+        pltpu.VMEM((2, half, rows, cols), BF),
+        pltpu.VMEM((chips - 1, rows, cols), BF),
+    ]
+
+
+def share_sum_steps(place, copies, mine, slots, column, result):
+    p = place
+    stage = mine[...]
+    partners = (p.sibling(), p.at(p.b1, p.z, p.c), p.at(p.b2, p.z, p.c))
+    for at, device in enumerate(partners):
+        slots[3 + at] = stage
+        copy = copies.start(slots.at[3 + at], slots.at[at], device)
+        yield
+        copy.wait_recv()
+        stage = stage + slots[at]
+    column[p.z] = stage
+    own = column.at[p.z]
+    along = [copies.start(own, own, p.at(p.b, p.along(k), p.c)) for k in range(1, p.chips)]
+    yield
+    for copy in along:
+        copy.wait_recv()
+    total = column[0]
+    for z in range(1, p.chips):
+        total = total + column[z]
+    result[...] = total
+
+
+SHARE_COPIES = 6
+
+
+def run_all(*steps):
+    live = list(steps)
+    while live:
+        for step in list(live):
+            try:
+                next(step)
+            except StopIteration:
+                live.remove(step)
+
+
+def gather_kernel(
+    groups, seqs, qkv_ref, proj_ref, up_ref, down_ref, norm_ref,
+    qkv_full, pu_full, down_full, norms_out, norm_full, send_sems, recv_sems,
+):
+    p = Place(groups, seqs)
+    width = proj_ref.shape[1]
+    b, z, c = p.b, p.z, p.c
+    index = b * seqs + 2 * z + c
+    qkv_full[b, z, c] = qkv_ref[...].astype(BF)
+    pu_full[b, z, c, :, :width] = proj_ref[...].astype(BF)
+    pu_full[b, z, c, :, width:] = up_ref[...].astype(BF)
+    down_full[b, z, c] = down_ref[...].astype(BF)
+    rows, piece = norm_ref.shape
+    per = LANES // piece
+    tiled = jnp.concatenate([norm_ref[...].astype(BF).astype(F32)] * per, axis=1)
+    lane = lax.broadcasted_iota(jnp.int32, tiled.shape, 1)
+    norm_full[b, z, c] = jnp.where(lane // piece == index % per, tiled, 0.0)
+    meet(p)
+    copies = Copies(send_sems, recv_sems)
+    run_all(*(gather_steps(p, copies, full) for full in (norm_full, qkv_full, pu_full, down_full)))
+    for block in range(norms_out.shape[1] // LANES):
+        total = None
+        for device in range(block * per, (block + 1) * per):
+            one = norm_full[device // seqs, device % seqs // 2, device % 2]
+            total = one if total is None else total + one
+        norms_out[:, block * LANES : (block + 1) * LANES] = total
+    copies.finish()
+
+
+def summary_gather_kernel(groups, seqs, own_ref, full_ref, send_sems, recv_sems):
+    p = Place(groups, seqs)
+    full_ref[p.z, p.c] = own_ref[...]
+    meet(p)
+    copies = Copies(send_sems, recv_sems)
+    own = full_ref.at[p.z, p.c]
+    along = [copies.start(own, own, p.at(p.b, p.along(k), p.c)) for k in range(1, p.chips)]
+    sib = [copies.start(own, own, p.sibling())]
+    for k, copy in enumerate(along):
+        copy.wait_recv()
+        block = full_ref.at[(p.z + p.chips - 1 - k) % p.chips, p.c]
+        sib.append(copies.start(block, block, p.sibling()))
+    for copy in sib:
+        copy.wait_recv()
+    copies.finish()
+
+
+def summary_scatter_kernel(groups, seqs, grad_ref, out_ref, got, low, last, send_sems, recv_sems):
+    p = Place(groups, seqs)
+    meet(p)
+    copies = Copies(send_sems, recv_sems)
+    swap = copies.start(grad_ref.at[:, p.other], got, p.sibling())
+    swap.wait_recv()
+    along = []
+    for k in range(1, p.chips):
+        to = p.along(k)
+        low[k - 1] = (grad_ref[to, p.c] + got[to]).astype(BF)
+        along.append(copies.start(low.at[k - 1], last.at[k - 1], p.at(p.b, to, p.c)))
+    total = grad_ref[p.z, p.c] + got[p.z]
+    for k, copy in enumerate(along):
+        copy.wait_recv()
+        total = total + last[k].astype(F32)
+    out_ref[...] = total
+    copies.finish()
+
+
+def reduce_kernel(
+    groups, seqs, qkv_ref, pu_ref, down_ref, norm_ref, qkv_out, pu_out, down_out, norm_out, total_out, *scratch
+):
+    *buffers, slots, column, sq_mine, sq_slots, sq_column, send_sems, recv_sems = scratch
+    p = Place(groups, seqs)
+    meet(p)
+    copies = Copies(send_sems, recv_sems)
+    steps = [share_sum_steps(p, copies, norm_ref, slots, column, norm_out)]
+    for at, (grad, out) in enumerate(((down_ref, down_out), (pu_ref, pu_out), (qkv_ref, qkv_out))):
+        steps.append(scatter_steps(p, copies, grad, *buffers[5 * at : 5 * at + 5], out))
+    run_all(*steps)
+    local = sum(jnp.sum(jnp.square(out[...]), keepdims=True) for out in (qkv_out, pu_out, down_out))
+    sq_mine[...] = jnp.broadcast_to(local, sq_mine.shape)
+    run_all(share_sum_steps(p, copies, sq_mine, sq_slots, sq_column, total_out))
+    total_out[...] = total_out[...] + jnp.sum(jnp.square(norm_out[...]), keepdims=True)
+    copies.finish()
+
+
+def adam(grad, master, first, second, rate, moment_out, square_out, fresh_out):
+    fix = 1.0 - BETA**STEP
+    moment = BETA * first + (1.0 - BETA) * grad
+    square = BETA * second + (1.0 - BETA) * grad * grad
+    update = moment / fix / (jnp.sqrt(square / fix) + ADAM_EPS)
+    moment_out[...] = moment
+    square_out[...] = square
+    fresh_out[...] = master - rate * (update + DECAY * master)
+
+
+def update_kernel(index_ref, total_ref, qkv_grad, pu_grad, down_grad, norm_grad, *refs):
+    state, outs = refs[:15], refs[15:]
+    norm_out, moments, squares, fresh = outs[0], outs[1:6], outs[6:11], outs[11:16]
+    grad_norm = jnp.sqrt(total_ref[0:1, 0:1])
+    norm_out[...] = grad_norm
+    factor = jnp.minimum(1.0, CLIP / (grad_norm + 1e-06))
+    width = state[1].shape[1]
+    piece = state[4].shape[1]
+    per = LANES // piece
+    index = index_ref[0]
+    block = norm_grad[:, pl.ds(pl.multiple_of(index // per * LANES, LANES), LANES)]
+    own = pltpu.roll(block, (LANES - index % per * piece) % LANES, 1)[:, :piece]
+    grads = (qkv_grad[...], pu_grad[:, :width], pu_grad[:, width:], down_grad[...], own)
+    for at, (grad, rate) in enumerate(zip(grads, RATES)):
+        adam(
+            grad * factor, state[at][...], state[5 + at][...], state[10 + at][...], rate,
+            moments[at], squares[at], fresh[at],
+        )
+    outs[16][...] = own[3:4] * factor
+
+
 def qkv_kernel(info_ref, x_ref, norms_ref, weight_ref, mixed_ref, summ_ref, sum_scr):
     step = pl.program_id(0)
     tile, width = x_ref.shape
@@ -218,18 +517,18 @@
 
 
 def mlp_kernel(
-    x_ref, attn_ref, og_ref, norms_ref, proj_ref, up_ref, down_ref,
-    out_ref, resid_grad_ref, attn_grad_ref, proj_grad_ref, up_grad_ref, down_grad_ref, norm_grad_ref,
+    x_ref, attn_ref, og_ref, norms_ref, pu_ref, down_ref,
+    out_ref, resid_grad_ref, attn_grad_ref, pu_grad_ref, down_grad_ref, norm_grad_ref,
     activ_scr, pre_grad_scr, n2t_scr, attnt_scr, ogt_scr, pig_scr, norm_scr,
 ):
     step = pl.program_id(0)
     tile, width = x_ref.shape
-    hidden = up_ref.shape[1]
+    hidden = down_ref.shape[0]
     rows = pl.ds(pl.multiple_of(step * tile, tile), tile)
     chunk = 512
     attn = attn_ref[...]
     grad = og_ref[...]
-    resid = x_ref[...].astype(F32) + dot(attn, proj_ref[...])
+    resid = x_ref[...].astype(F32) + dot(attn, pu_ref[:, :width])
     xhat, rstd = normalize(resid)
     gain = norms_ref[2:3, :]
     normed = (xhat * gain + norms_ref[3:4, :]).astype(BF)
@@ -239,7 +538,7 @@
     acc = resid
     back = jnp.zeros_like(resid)
     for at in range(0, hidden, chunk):
-        pre = dot(normed, up_ref[:, at : at + chunk])
+        pre = dot(normed, pu_ref[:, width + at : width + at + chunk])
         act_grad = dot_nt(grad, down_ref[at : at + chunk, :])
         value, slope = gelu_parts(pre)
         activ = value.astype(BF)
@@ -247,13 +546,13 @@
         activ_scr[rows, at : at + chunk] = activ
         pre_grad_scr[rows, at : at + chunk] = pre_grad
         acc = acc + dot(activ, down_ref[at : at + chunk, :])
-        back = back + dot_nt(pre_grad, up_ref[:, at : at + chunk])
+        back = back + dot_nt(pre_grad, pu_ref[:, width + at : width + at + chunk])
     out_ref[...] = acc.astype(BF)
     resid_grad = grad.astype(F32) + norm_back(back, gain, xhat, rstd)
     resid_grad_ref[...] = resid_grad
     pig = resid_grad.astype(BF)
     pig_scr[rows, :] = pig
-    attn_grad_ref[...] = dot_nt(pig, proj_ref[...]).astype(BF)
+    attn_grad_ref[...] = dot_nt(pig, pu_ref[:, :width]).astype(BF)
     gain_part = jnp.sum(back * xhat, axis=0, keepdims=True)
     shift_part = jnp.sum(back, axis=0, keepdims=True)
     part = jnp.concatenate([gain_part, shift_part], axis=0)
@@ -269,13 +568,14 @@
     @pl.when(step == pl.num_programs(0) - 1)
     def _():
         norm_grad_ref[...] = norm_scr[...]
-        proj_grad_ref[...] = dot(attnt_scr[...], pig_scr[...])
+        pu_grad_ref[:, :width] = dot(attnt_scr[...], pig_scr[...]).astype(BF)
         cols = 256
 
         def one(index, carry):
             c = pl.ds(pl.multiple_of(index * cols, cols), cols)
-            up_grad_ref[:, c] = dot(n2t_scr[...], pre_grad_scr[:, c])
-            down_grad_ref[c, :] = dot(ogt_scr[...], activ_scr[:, c]).T
+            out = pl.ds(pl.multiple_of(width + index * cols, cols), cols)
+            pu_grad_ref[:, out] = dot(n2t_scr[...], pre_grad_scr[:, c]).astype(BF)
+            down_grad_ref[c, :] = dot(ogt_scr[...], activ_scr[:, c]).T.astype(BF)
             return carry
 
         lax.fori_loop(0, hidden // cols, one, 0)
@@ -326,7 +626,7 @@
 
         def one(index, carry):
             c = pl.ds(pl.multiple_of(index * cols, cols), cols)
-            qkv_grad_ref[:, c] = dot(n1t_scr[...], mg_scr[:, c])
+            qkv_grad_ref[:, c] = dot(n1t_scr[...], mg_scr[:, c]).astype(BF)
             return carry
 
         lax.fori_loop(0, qkv_grad_ref.shape[1] // cols, one, 0)
@@ -342,6 +642,19 @@
 
 SCALARS = pl.BlockSpec(memory_space=pltpu.SMEM)
 PARAMS = pltpu.CompilerParams(vmem_limit_bytes=VMEM_LIMIT)
+
+
+def remote_call(kernel, groups, seqs, name, collective_id, out_shape, scratch, copies):
+    return pl.pallas_call(
+        functools.partial(kernel, groups, seqs),
+        out_shape=out_shape,
+        scratch_shapes=list(scratch)
+        + [pltpu.SemaphoreType.DMA((copies,)), pltpu.SemaphoreType.DMA((copies,))],
+        compiler_params=pltpu.CompilerParams(
+            vmem_limit_bytes=VMEM_LIMIT, collective_id=collective_id, has_side_effects=True
+        ),
+        name=name,
+    )
 
 
 def regroup(grad, dim, outer, inner):
@@ -351,29 +664,57 @@
     return jnp.swapaxes(split, dim, dim + 1).reshape(shape)
 
 
-def body(
-    inputs, out_grad, lengths, qkv_weight, proj_weight, up_weight, down_weight, norm_params,
-    qkv_mean, proj_mean, up_mean, down_mean, norm_mean,
-    qkv_second, proj_second, up_second, down_second, norm_second,
-):
+def gather_plain(state):
     both = ("batch", "seq")
-    gather = lambda w, axis: lax.all_gather(w.astype(BF), both, axis=axis, tiled=True)
-    qkv_full = gather(qkv_weight, 0)
-    proj_full = gather(proj_weight, 0)
-    up_full = gather(up_weight, 0)
-    down_full = gather(down_weight, 0)
-    norms = gather(norm_params, 1).astype(F32)
+    qkv, proj, up, down = (lax.all_gather(w.astype(BF), both, axis=0, tiled=True) for w in state[:4])
+    norms = lax.all_gather(state[4].astype(BF), both, axis=1, tiled=True).astype(F32)
+    return qkv, jnp.concatenate([proj, up], axis=1), down, norms
+
+
+def reduce_plain(qkv_grad, pu_grad, down_grad, norm_grad):
+    groups, seqs = lax.axis_size("batch"), lax.axis_size("seq")
+    reduced = []
+    for grad, dim in ((qkv_grad, 0), (pu_grad, 0), (down_grad, 0)):
+        part = lax.psum_scatter(
+            regroup(grad.astype(F32), dim, groups, seqs), "seq", scatter_dimension=dim, tiled=True
+        )
+        reduced.append(lax.psum_scatter(part, "batch", scatter_dimension=dim, tiled=True))
+    norm_total = lax.psum(norm_grad, ("batch", "seq"))
+    squares = lax.psum(sum(jnp.sum(grad * grad) for grad in reduced), ("batch", "seq"))
+    squares = squares + jnp.sum(norm_total * norm_total)
+    return (*reduced, norm_total, jnp.broadcast_to(squares, (8, LANES)))
+
+
+def body(groups, seqs, inputs, out_grad, lengths, *state):
+    sds = jax.ShapeDtypeStruct
     rows, width = inputs.shape[1], inputs.shape[2]
-    hidden = up_full.shape[1]
+    own_rows, down_rows = state[0].shape[0], state[3].shape[0]
+    hidden = state[2].shape[1]
+    chips = seqs // 2
+    direct = groups == 4 and seqs % 4 == 0 and own_rows % 16 == 0
+    grid3 = (groups, chips, 2)
+    if direct:
+        qkv_full, pu_full, down_full, norms = remote_call(
+            gather_kernel, groups, seqs, "gather", 0,
+            [
+                sds((*grid3, own_rows, 3 * width), BF), sds((*grid3, own_rows, width + hidden), BF),
+                sds((*grid3, down_rows, width), BF), sds((4, width), F32),
+            ],
+            [pltpu.VMEM((*grid3, 4, LANES), F32)], 4 * GATHER_COPIES,
+        )(*state[:5])
+        qkv_full = qkv_full.reshape(width, 3 * width)
+        pu_full = pu_full.reshape(width, width + hidden)
+        down_full = down_full.reshape(hidden, width)
+    else:
+        qkv_full, pu_full, down_full, norms = gather_plain(state[:5])
     local = rows // SPAN
-    spans = local * lax.axis_size("seq")
+    spans = local * seqs
     first_span = lax.axis_index("seq") * local
     length = lengths[0]
     info = jnp.stack([length, first_span.astype(jnp.int32)])
     x, grad_rows = inputs[0], out_grad[0]
     tile = 256
     steps = rows // tile
-    sds = jax.ShapeDtypeStruct
     mixed, own_summ = pl.pallas_call(
         qkv_kernel,
         grid=(steps,),
@@ -384,7 +725,13 @@
         compiler_params=PARAMS,
         name="qkv",
     )(info, x, norms, qkv_full)
-    summ = lax.all_gather(own_summ, "seq", axis=0, tiled=True)
+    if direct:
+        summ = remote_call(
+            summary_gather_kernel, groups, seqs, "summary_gather", 1,
+            sds((chips, 2, local, 2 * width), BF), [], 2 * chips,
+        )(own_summ).reshape(spans, 2 * width)
+    else:
+        summ = lax.all_gather(own_summ, "seq", axis=0, tiled=True)
     pairs = width // LANES
     lse_spec = pl.BlockSpec((1, pairs, 2 * SPAN), lambda i: (i, 0, 0))
     attn_out, lse = pl.pallas_call(
@@ -397,17 +744,16 @@
         compiler_params=PARAMS,
         name="attend",
     )(info, mixed, summ)
-    outputs, resid_grad, attn_grad, proj_grad, up_grad, down_grad, norm_two = pl.pallas_call(
+    outputs, resid_grad, attn_grad, pu_grad, down_grad, norm_two = pl.pallas_call(
         mlp_kernel,
         grid=(steps,),
         in_specs=[by_rows(tile, width)] * 3
-        + [whole(norms.shape), whole(proj_full.shape), whole(up_full.shape), whole(down_full.shape)],
+        + [whole(norms.shape), whole(pu_full.shape), whole(down_full.shape)],
         out_specs=[by_rows(tile, width)] * 3
-        + [whole(proj_full.shape), whole(up_full.shape), whole(down_full.shape), whole((2, width))],
+        + [whole(pu_full.shape), whole(down_full.shape), whole((2, width))],
         out_shape=[
             sds((rows, width), BF), sds((rows, width), F32), sds((rows, width), BF),
-            sds(proj_full.shape, F32), sds(up_full.shape, F32), sds(down_full.shape, F32),
-            sds((2, width), F32),
+            sds(pu_full.shape, BF), sds(down_full.shape, BF), sds((2, width), F32),
         ],
         scratch_shapes=[
             pltpu.VMEM((rows, hidden), BF), pltpu.VMEM((rows, hidden), BF),
@@ -416,7 +762,7 @@
         ],
         compiler_params=PARAMS,
         name="mlp",
-    )(x, attn_out, grad_rows, norms, proj_full, up_full, down_full)
+    )(x, attn_out, grad_rows, norms, pu_full, down_full)
     dq, dkv, dsumm = pl.pallas_call(
         attend_back_kernel,
         grid=(local,),
@@ -427,7 +773,18 @@
         compiler_params=PARAMS,
         name="attend_back",
     )(info, mixed, attn_grad, lse, summ)
-    extra = lax.psum_scatter(dsumm, "seq", scatter_dimension=0, tiled=True)
+    if direct:
+        block = (local, 2 * width)
+        extra = remote_call(
+            summary_scatter_kernel, groups, seqs, "summary_scatter", 2, sds(block, F32),
+            [
+                pltpu.VMEM((chips, *block), F32), pltpu.VMEM((chips - 1, *block), BF),
+                pltpu.VMEM((chips - 1, *block), BF),
+            ],
+            chips,
+        )(dsumm.reshape(chips, 2, *block))
+    else:
+        extra = lax.psum_scatter(dsumm, "seq", scatter_dimension=0, tiled=True)
     input_grad, qkv_grad, norm_one = pl.pallas_call(
         final_kernel,
         grid=(steps,),
@@ -436,7 +793,7 @@
             whole(extra.shape), by_rows(tile, width), whole(norms.shape), whole(qkv_full.shape),
         ],
         out_specs=[by_rows(tile, width), whole(qkv_full.shape), whole((2, width))],
-        out_shape=[sds((rows, width), F32), sds(qkv_full.shape, F32), sds((2, width), F32)],
+        out_shape=[sds((rows, width), F32), sds(qkv_full.shape, BF), sds((2, width), F32)],
         scratch_shapes=[
             pltpu.VMEM((rows, 3 * width), BF), pltpu.VMEM((width, rows), BF), pltpu.VMEM((2, width), F32),
         ],
@@ -444,34 +801,35 @@
         name="final",
     )(info, x, dq, dkv, extra, resid_grad, norms, qkv_full)
     norm_grad = jnp.concatenate([norm_one, norm_two], axis=0)
-    groups = lax.axis_size("batch")
-    seq_count = lax.axis_size("seq")
-    reduced = []
-    for grad, dim in ((qkv_grad, 0), (proj_grad, 0), (up_grad, 0), (down_grad, 0), (norm_grad, 1)):
-        part = lax.psum_scatter(
-            regroup(grad, dim, groups, seq_count), "seq", scatter_dimension=dim, tiled=True
+    if direct:
+        shapes = ((down_rows, width), (own_rows, width + hidden), (own_rows, 3 * width))
+        scratch = [buffer for shape in shapes for buffer in scatter_scratch(groups, chips, *shape)]
+        scratch += [
+            pltpu.VMEM((6, 4, width), F32), pltpu.VMEM((chips, 4, width), F32),
+            pltpu.VMEM((8, LANES), F32), pltpu.VMEM((6, 8, LANES), F32), pltpu.VMEM((chips, 8, LANES), F32),
+        ]
+        reduced = remote_call(
+            reduce_kernel, groups, seqs, "reduce", 3,
+            [sds(shape, F32) for shape in (*reversed(shapes), (4, width), (8, LANES))],
+            scratch, 3 * SCATTER_COPIES + 2 * SHARE_COPIES,
+        )(
+            qkv_grad.reshape(*grid3, own_rows, 3 * width),
+            pu_grad.reshape(*grid3, own_rows, width + hidden),
+            down_grad.reshape(*grid3, down_rows, width), norm_grad,
         )
-        reduced.append(lax.psum_scatter(part, "batch", scatter_dimension=dim, tiled=True))
-    local_squares = sum((jnp.sum(grad * grad) for grad in reduced))
-    grad_norm = jnp.sqrt(lax.psum(local_squares, both))
-    factor = jnp.minimum(1.0, CLIP / (grad_norm + 1e-06))
-    fix = 1.0 - BETA**STEP
-    masters = (qkv_weight, proj_weight, up_weight, down_weight, norm_params)
-    firsts = (qkv_mean, proj_mean, up_mean, down_mean, norm_mean)
-    seconds = (qkv_second, proj_second, up_second, down_second, norm_second)
-    moments, squares, fresh = ([], [], [])
-    for grad, master, first, second, rate in zip(reduced, masters, firsts, seconds, RATES):
-        clipped = grad * factor
-        moment = BETA * first + (1.0 - BETA) * clipped
-        square = BETA * second + (1.0 - BETA) * clipped * clipped
-        update = moment / fix / (jnp.sqrt(square / fix) + ADAM_EPS)
-        moments.append(moment)
-        squares.append(square)
-        fresh.append(master - rate * (update + DECAY * master))
-    shift_clipped = reduced[4][3] * factor
-    return (
-        outputs[None], input_grad[None], grad_norm, *moments, *squares, *fresh, shift_clipped,
-    )
+    else:
+        reduced = reduce_plain(qkv_grad, pu_grad, down_grad, norm_grad)
+    *grads, norm_total, total = reduced
+    index = lax.axis_index("batch") * seqs + lax.axis_index("seq")
+    owned = [sds(w.shape, F32) for w in state[:5]]
+    grad_norm, *fresh, shift_clipped = pl.pallas_call(
+        update_kernel,
+        in_specs=[SCALARS] + [pl.BlockSpec(memory_space=pltpu.VMEM)] * 20,
+        out_shape=[sds((1, 1), F32), *owned, *owned, *owned, sds((1, state[4].shape[1]), F32)],
+        compiler_params=PARAMS,
+        name="update",
+    )(index.astype(jnp.int32)[None], total, *grads, norm_total, *state)
+    return (outputs[None], input_grad[None], grad_norm[0, 0], *fresh, shift_clipped[0])
 
 
 def solution(mesh):
@@ -480,7 +838,7 @@
     columns = P(None, ("batch", "seq"))
     state = (owned, owned, owned, owned, columns)
     return jax.shard_map(
-        body,
+        functools.partial(body, mesh.shape["batch"], mesh.shape["seq"]),
         mesh=mesh,
         in_specs=(tokens, tokens, P("batch")) + state * 3,
         out_specs=(tokens, tokens, P()) + state * 3 + (P(("batch", "seq")),),

time: 670 us -> 264 us (0.39)
  waiting for transfers between devices: 326 us -> 0 us
  blocking collectives: 151 us -> 0 us
  Pallas kernels: 131 us -> 260 us
  between operations: 20.6 us -> 1.37 us
  other arithmetic: 20.9 us -> 1.88 us
  local copies, waits for them, and re-layouts: 18.5 us -> 0.01 us
    reduce_scatter x9 -> x0, waiting for transfers between devices: 259 us -> none  [the longest x4 141 us: body(): lax.psum_scatter(regroup(grad, dim, groups, seq_count), 'seq', scatter_di...]
    pallas_call x0 -> x5, Pallas kernels: none -> 131 us  [the longest x1 60.7 us: body(): remote_call(reduce_kernel, groups, seqs, 'reduce', 3, [sds(shape, F32) fo...]
    all_gather x3 -> x0, blocking collectives: 102 us -> none  [the longest x2 85.4 us: body(): lax.all_gather(w.astype(BF), both, axis=axis, tiled=True)]
    psum x1 -> x0, blocking collectives: 39.3 us -> none  [body(): grad_norm = jnp.sqrt(lax.psum(local_squares, both))]
    all_gather x3 -> x0, waiting for transfers between devices: 35.9 us -> none  [body(): lax.all_gather(w.astype(BF), both, axis=axis, tiled=True)]
    unnamed x14 -> x0, waiting for transfers between devices: 30.3 us -> none
    transpose x4 -> x0, local copies, waits for them, and re-layouts: 14.6 us -> none  [regroup(): return jnp.swapaxes(split, dim, dim + 1).reshape(shape)]
    unnamed x1 -> x0, blocking collectives: 9.79 us -> none
  transfers between devices with their start and end apart: 13 -> 0, of which waited for: 10 -> 0; matrix products, arithmetic and copies ran while one was open for 4% -> 0% of each run, Pallas kernels for 8% -> 0%
where the time goes in v2:
time: 264 us; the launch traced here: 263 us
  Pallas kernels  260 us (98%)
    pallas_call x1, Pallas kernels, body(): remote_call(reduce_kernel, groups, seqs, 'reduce', 3, [sds(shape, F32) fo...  60.7 us
    pallas_call x1, Pallas kernels, body(): pl.pallas_call(mlp_kernel, grid=(steps,), in_specs=[by_rows(tile, width)]...  48.2 us
    pallas_call x1, Pallas kernels, body(): remote_call(gather_kernel, groups, seqs, 'gather', 0, [sds((*grid3, own_r...  46 us
    pallas_call x1, Pallas kernels, body(): pl.pallas_call(attend_back_kernel, grid=(local,), in_specs=[SCALARS, by_r...  28.6 us
    pallas_call x1, Pallas kernels, body(): pl.pallas_call(attend_kernel, grid=(local,), in_specs=[SCALARS, by_rows(S...  24.3 us
    pallas_call x1, Pallas kernels, body(): pl.pallas_call(final_kernel, grid=(steps,), in_specs=[SCALARS, by_rows(ti...  17.7 us
    pallas_call x1, Pallas kernels, body(): remote_call(summary_scatter_kernel, groups, seqs, 'summary_scatter', 2, s...  10.6 us
    pallas_call x1, Pallas kernels, body(): remote_call(summary_gather_kernel, groups, seqs, 'summary_gather', 1, sds...  10.4 us

profile of v2, /device:TPU:0, one launch (start us, length us, event | category | flops | bytes accessed | tf_op | source)
XLA Modules:
  0.0 262.9 jit_solution(3257043720155434402)
XLA Ops:
  1.3 0.6 pad_add_fusion.info_ref
  1.9 46.0 %gather.1 = (bf16[4,4,2,16,1536]{4,3,2,1,0:T(8,128)(2,1)}, bf16[4,4,2,16,2560]{4,3,2,1,0:T(8,128)(2,1)}, bf16[4,4,2,64,512]{4,3,2,1,0:T(8,128)(2,1)}, f32[4,512]{1,0:T(4,128)}) custom-call(f32[16,1536]{1,0:T(8,128)} %refs_0_.1, f32[16,512]{1,0:T(8,128)} %refs_1_.1, f32[16,2048]{1,0:T(8,128)} %refs_2_.1, f32[64,512]{1,0:T(8,128)} %refs_3_.1, f32[4,16]{1,0:T(4,128)} %refs_4_.1), custom_call_target="tpu_custom_call" | custom-call | tf_op jit(solution)/shard_map/gather/pallas_call | solution.py:697
  47.9 10.2 %qkv.1 = (bf16[2048,1536]{1,0:T(8,128)(2,1)}, bf16[16,1024]{1,0:T(8,128)(2,1)}) custom-call(s32[2]{0:T(128)} %pad_add_fusion.info_ref, bf16[2048,512]{1,0:T(8,128)(2,1)} %bitcast.16, f32[4,512]{1,0:T(4,128)} %get-tuple-element.61.norms_ref, bf16[512,1536]{1,0:T(8,128)(2,1)} %bitcast.19), custom_call_target="tpu_custom_call" | custom-call | tf_op jit(solution)/shard_map/qkv/pallas_call | solution.py:718
  58.1 10.4 %summary_gather.1 = bf16[4,2,16,1024]{3,2,1,0:T(8,128)(2,1)} custom-call(bf16[16,1024]{1,0:T(8,128)(2,1)} %get-tuple-element.64.own_ref), custom_call_target="tpu_custom_call" | custom-call | tf_op jit(solution)/shard_map/summary_gather/pallas_call | solution.py:729
  68.6 24.3 %attend.1 = (bf16[2048,512]{1,0:T(8,128)(2,1)}, f32[16,4,256]{2,1,0:T(4,128)}) custom-call(s32[2]{0:T(128)} %pad_add_fusion.info_ref, bf16[2048,1536]{1,0:T(8,128)(2,1)} %get-tuple-element.63.mixed_ref, bf16[128,1024]{1,0:T(8,128)(2,1)} %bitcast.23), custom_call_target="tpu_custom_call" | custom-call | tf_op jit(solution)/shard_map/attend/pallas_call | solution.py:737
  92.9 48.2 %mlp.1 = (bf16[2048,512]{1,0:T(8,128)(2,1)}, f32[2048,512]{1,0:T(8,128)}, bf16[2048,512]{1,0:T(8,128)(2,1)}, bf16[512,2560]{1,0:T(8,128)(2,1)}, bf16[2048,512]{1,0:T(8,128)(2,1)}, /*index=5*/f32[2,512]{1,0:T(2,128)}) custom-call(bf16[2048,512]{1,0:T(8,128)(2,1)} %bitcast.17, bf16[2048,512]{1,0:T(8,128)(2,1)} %get-tuple-element.65.attn_ref, ...), custom_call_target="tpu_custom_call" | custom-call | tf_op jit(solution)/shard_map/mlp/pallas_call | solution.py:747
  141.1 28.6 %attend_back.1 = (bf16[2048,512]{1,0:T(8,128)(2,1)}, f32[2048,1024]{1,0:T(8,128)}, f32[128,1024]{1,0:T(8,128)}) custom-call(s32[2]{0:T(128)} %pad_add_fusion.info_ref, bf16[2048,1536]{1,0:T(8,128)(2,1)} %get-tuple-element.63.mixed_ref, bf16[2048,512]{1,0:T(8,128)(2,1)} %get-tuple-element.69.grad_ref, f32[16,4,256]{2,1,0:T(4,128)} %get-tuple-element.70.lse_ref, ...), custom_call_target="tpu_custom_call" | custom-call | tf_op jit(solution)/shard_map/attend_back/pallas_call | solution.py:766
  169.7 10.6 %summary_scatter.1.extra_ref = f32[16,1024]{1,0:T(8,128)} custom-call(f32[4,2,16,1024]{3,2,1,0:T(8,128)} %bitcast.29), custom_call_target="tpu_custom_call" | custom-call | tf_op jit(solution)/shard_map/summary_scatter/pallas_call | solution.py:778
  180.3 0.0 copy-start
  180.3 17.7 %final.1 = (f32[2048,512]{1,0:T(8,128)}, bf16[512,1536]{1,0:T(8,128)(2,1)}, f32[2,512]{1,0:T(2,128)}) custom-call(s32[2]{0:T(128)} %pad_add_fusion.info_ref, bf16[2048,512]{1,0:T(8,128)(2,1)} %bitcast.18, bf16[2048,512]{1,0:T(8,128)(2,1)} %get-tuple-element.71.dq_ref, f32[2048,1024]{1,0:T(8,128)} %get-tuple-element.72.dkv_ref, ...), custom_call_target="tpu_custom_call" | custom-call | tf_op jit(solution)/shard_map/final/pallas_call | solution.py:788
  198.1 0.0 copy-done
  198.1 1.3 pad_maximum_fusion.norm_ref
  199.4 60.7 %reduce.1 = (f32[16,1536]{1,0:T(8,128)}, f32[16,2560]{1,0:T(8,128)}, f32[64,512]{1,0:T(8,128)}, f32[4,512]{1,0:T(4,128)}, f32[8,128]{1,0:T(8,128)}) custom-call(bf16[4,4,2,16,1536]{4,3,2,1,0:T(8,128)(2,1)} %bitcast.28, bf16[4,4,2,16,2560]{4,3,2,1,0:T(8,128)(2,1)} %bitcast.21, bf16[4,4,2,64,512]{4,3,2,1,0:T(8,128)(2,1)} %bitcast.25, ...), custom_call_target="tpu_custom_call" | custom-call | tf_op jit(solution)/shard_map/reduce/pallas_call | solution.py:811
  260.1 2.8 %update.1 = (f32[1,1]{1,0:T(1,128)}, f32[16,1536]{1,0:T(8,128)}, f32[16,512]{1,0:T(8,128)}, f32[16,2048]{1,0:T(8,128)}, f32[64,512]{1,0:T(8,128)}, /*index=5*/f3...) custom-call(s32[1]{0:T(128)} %bitcast.10.index_ref, ...), custom_call_target="tpu_custom_call" | custom-call | tf_op jit(solution)/shard_map/update/pallas_call | solution.py:825
Async XLA Ops:
  180.3 17.8 %copy-start = (f32[2,512]{1,0:T(2,128)S(1)}, f32[2,512]{1,0:T(2,128)}, u32[]{:S(2)}) copy-start(f32[2,512]{1,0:T(2,128)} %get-tuple-element.80) | copy-start | bytes 12292

commit v3 on v2

--- a/solution.py
+++ b/solution.py
@@ -352,89 +352,6 @@
                 live.remove(step)
 
 
-def gather_kernel(
-    groups, seqs, qkv_ref, proj_ref, up_ref, down_ref, norm_ref,
-    qkv_full, pu_full, down_full, norms_out, norm_full, send_sems, recv_sems,
-):
-    p = Place(groups, seqs)
-    width = proj_ref.shape[1]
-    b, z, c = p.b, p.z, p.c
-    index = b * seqs + 2 * z + c
-    qkv_full[b, z, c] = qkv_ref[...].astype(BF)
-    pu_full[b, z, c, :, :width] = proj_ref[...].astype(BF)
-    pu_full[b, z, c, :, width:] = up_ref[...].astype(BF)
-    down_full[b, z, c] = down_ref[...].astype(BF)
-    rows, piece = norm_ref.shape
-    per = LANES // piece
-    tiled = jnp.concatenate([norm_ref[...].astype(BF).astype(F32)] * per, axis=1)
-    lane = lax.broadcasted_iota(jnp.int32, tiled.shape, 1)
-    norm_full[b, z, c] = jnp.where(lane // piece == index % per, tiled, 0.0)
-    meet(p)
-    copies = Copies(send_sems, recv_sems)
-    run_all(*(gather_steps(p, copies, full) for full in (norm_full, qkv_full, pu_full, down_full)))
-    for block in range(norms_out.shape[1] // LANES):
-        total = None
-        for device in range(block * per, (block + 1) * per):
-            one = norm_full[device // seqs, device % seqs // 2, device % 2]
-            total = one if total is None else total + one
-        norms_out[:, block * LANES : (block + 1) * LANES] = total
-    copies.finish()
-
-
-def summary_gather_kernel(groups, seqs, own_ref, full_ref, send_sems, recv_sems):
-    p = Place(groups, seqs)
-    full_ref[p.z, p.c] = own_ref[...]
-    meet(p)
-    copies = Copies(send_sems, recv_sems)
-    own = full_ref.at[p.z, p.c]
-    along = [copies.start(own, own, p.at(p.b, p.along(k), p.c)) for k in range(1, p.chips)]
-    sib = [copies.start(own, own, p.sibling())]
-    for k, copy in enumerate(along):
-        copy.wait_recv()
-        block = full_ref.at[(p.z + p.chips - 1 - k) % p.chips, p.c]
-        sib.append(copies.start(block, block, p.sibling()))
-    for copy in sib:
-        copy.wait_recv()
-    copies.finish()
-
-
-def summary_scatter_kernel(groups, seqs, grad_ref, out_ref, got, low, last, send_sems, recv_sems):
-    p = Place(groups, seqs)
-    meet(p)
-    copies = Copies(send_sems, recv_sems)
-    swap = copies.start(grad_ref.at[:, p.other], got, p.sibling())
-    swap.wait_recv()
-    along = []
-    for k in range(1, p.chips):
-        to = p.along(k)
-        low[k - 1] = (grad_ref[to, p.c] + got[to]).astype(BF)
-        along.append(copies.start(low.at[k - 1], last.at[k - 1], p.at(p.b, to, p.c)))
-    total = grad_ref[p.z, p.c] + got[p.z]
-    for k, copy in enumerate(along):
-        copy.wait_recv()
-        total = total + last[k].astype(F32)
-    out_ref[...] = total
-    copies.finish()
-
-
-def reduce_kernel(
-    groups, seqs, qkv_ref, pu_ref, down_ref, norm_ref, qkv_out, pu_out, down_out, norm_out, total_out, *scratch
-):
-    *buffers, slots, column, sq_mine, sq_slots, sq_column, send_sems, recv_sems = scratch
-    p = Place(groups, seqs)
-    meet(p)
-    copies = Copies(send_sems, recv_sems)
-    steps = [share_sum_steps(p, copies, norm_ref, slots, column, norm_out)]
-    for at, (grad, out) in enumerate(((down_ref, down_out), (pu_ref, pu_out), (qkv_ref, qkv_out))):
-        steps.append(scatter_steps(p, copies, grad, *buffers[5 * at : 5 * at + 5], out))
-    run_all(*steps)
-    local = sum(jnp.sum(jnp.square(out[...]), keepdims=True) for out in (qkv_out, pu_out, down_out))
-    sq_mine[...] = jnp.broadcast_to(local, sq_mine.shape)
-    run_all(share_sum_steps(p, copies, sq_mine, sq_slots, sq_column, total_out))
-    total_out[...] = total_out[...] + jnp.sum(jnp.square(norm_out[...]), keepdims=True)
-    copies.finish()
-
-
 def adam(grad, master, first, second, rate, moment_out, square_out, fresh_out):
     fix = 1.0 - BETA**STEP
     moment = BETA * first + (1.0 - BETA) * grad
@@ -464,6 +381,261 @@
             moments[at], squares[at], fresh[at],
         )
     outs[16][...] = own[3:4] * factor
+
+
+def tick(*steps):
+    for step in steps:
+        next(step, None)
+
+
+def cast_shards(p, seqs, qkv_ref, proj_ref, up_ref, down_ref, norm_ref, qkv_full, pu_full, down_full, norm_full):
+    width = proj_ref.shape[1]
+    b, z, c = p.b, p.z, p.c
+    index = b * seqs + 2 * z + c
+    qkv_full[b, z, c] = qkv_ref[...].astype(BF)
+    pu_full[b, z, c, :, :width] = proj_ref[...].astype(BF)
+    pu_full[b, z, c, :, width:] = up_ref[...].astype(BF)
+    down_full[b, z, c] = down_ref[...].astype(BF)
+    piece = norm_ref.shape[1]
+    per = LANES // piece
+    tiled = jnp.concatenate([norm_ref[...].astype(BF).astype(F32)] * per, axis=1)
+    lane = lax.broadcasted_iota(jnp.int32, tiled.shape, 1)
+    norm_full[b, z, c] = jnp.where(lane // piece == index % per, tiled, 0.0)
+
+
+def join_norms(norm_full, seqs, per, norms_out):
+    for block in range(norms_out.shape[1] // LANES):
+        total = None
+        for device in range(block * per, (block + 1) * per):
+            one = norm_full[device // seqs, device % seqs // 2, device % 2]
+            total = one if total is None else total + one
+        norms_out[:, block * LANES : (block + 1) * LANES] = total
+
+
+def tiles(first, last, size, one):
+    def step(index, carry):
+        one(pl.multiple_of(index * size, size), index)
+        return carry
+
+    lax.fori_loop(first, last, step, 0)
+
+
+def front_kernel(
+    groups, seqs, info_ref, x_ref, qkv_ref, proj_ref, up_ref, down_ref, norm_ref,
+    qkv_full, pu_full, down_full, norms_out, mixed_ref, summ_ref, attn_ref, lse_ref,
+    norm_full, xhat_scr, sum_scr, vt_scr, send_sems, recv_sems,
+):
+    p = Place(groups, seqs)
+    rows, width = x_ref.shape
+    local = rows // SPAN
+    length, first_span = info_ref[0], info_ref[1]
+    cast_shards(
+        p, seqs, qkv_ref, proj_ref, up_ref, down_ref, norm_ref, qkv_full, pu_full, down_full, norm_full
+    )
+    meet(p)
+    copies = Copies(send_sems, recv_sems)
+    in_norm, in_qkv, in_pu, in_down = (
+        gather_steps(p, copies, full) for full in (norm_full, qkv_full, pu_full, down_full)
+    )
+    tile = 256
+    count = rows // tile
+
+    def center(at, index):
+        xhat_scr[pl.ds(at, tile), :] = normalize(x_ref[pl.ds(at, tile), :].astype(F32))[0]
+
+    tick(in_norm, in_qkv)
+    tiles(0, count // 4, tile, center)
+    tick(in_norm, in_qkv, in_pu)
+    tiles(count // 4, count // 2, tile, center)
+    tick(in_norm, in_qkv)
+    tiles(count // 2, count, tile, center)
+    tick(in_norm, in_qkv)
+    tick(in_norm, in_qkv)
+    join_norms(norm_full, seqs, LANES // norm_ref.shape[1], norms_out)
+    gain, shift = norms_out[0:1, :], norms_out[1:2, :]
+
+    def weight(begin, size):
+        return qkv_full[:, :, :, :, begin : begin + size].reshape(width, size)
+
+    def normed_of(at):
+        return (xhat_scr[pl.ds(at, tile), :] * gain + shift).astype(BF)
+
+    def keys_values(at, index):
+        mixed = dot(normed_of(at), weight(width, 2 * width)).astype(BF)
+        mixed_ref[pl.ds(at, tile), width:] = mixed
+        for part in range(tile // SPAN):
+            span = index * (tile // SPAN) + part
+            sum_scr[pl.ds(span, 1), :] = span_sum(
+                mixed[part * SPAN : (part + 1) * SPAN], length, (first_span + span) * SPAN
+            )
+
+    def queries(at, index):
+        mixed_ref[pl.ds(at, tile), :width] = dot(normed_of(at), weight(0, width)).astype(BF)
+
+    tiles(0, count // 2, tile, keys_values)
+    tick(in_pu, in_down)
+    tiles(count // 2, count, tile, keys_values)
+    summ_ref[p.z, p.c] = sum_scr[...].astype(BF)
+    own = summ_ref.at[p.z, p.c]
+    along = [copies.start(own, own, p.at(p.b, p.along(k), p.c)) for k in range(1, p.chips)]
+    sib = [copies.start(own, own, p.sibling())]
+    tiles(0, count, tile, queries)
+    for k, copy in enumerate(along):
+        copy.wait_recv()
+        block = summ_ref.at[(p.z + p.chips - 1 - k) % p.chips, p.c]
+        sib.append(copies.start(block, block, p.sibling()))
+    tick(in_pu)
+    for copy in sib:
+        copy.wait_recv()
+    summ = summ_ref[...].reshape(local * seqs, 2 * width)
+    vt_scr[...] = summ[:, width:].T
+    summ_rows = SummaryView(summ_ref, local * seqs)
+
+    def attend(at, index):
+        caps = span_caps(length, first_span + index)
+
+        def keep(pair, value):
+            lse_ref[index, pair : pair + 1, :] = value
+
+        attend_span(mixed_ref, at, width, summ_rows, vt_scr, caps, attn_ref, at, keep)
+
+    for part in range(4):
+        tiles(part * local // 4, (part + 1) * local // 4, SPAN, attend)
+        tick(in_down, in_pu)
+    tick(in_down, in_pu)
+    copies.finish()
+
+
+class SummaryView:
+    def __init__(self, ref, rows):
+        self.ref, self.rows = ref, rows
+
+    def __getitem__(self, key):
+        cols = key[1]
+        return self.ref[:, :, :, cols].reshape(self.rows, cols.stop - cols.start)
+
+
+def back_kernel(
+    groups, seqs, info_ref, x_ref, mixed_ref, grad_ref, lse_ref, summ_ref, resid_grad_ref, pu_ref, down_ref,
+    norms_ref, weight_ref, norm_two_ref,
+    input_grad_ref, qkv_out, pu_out, down_out, norm_out, total_out,
+    mg_scr, dkv_scr, n1t_scr, kt_scr, dsumm_scr, dsumm_got, dsumm_low, dsumm_last, extra_scr, q_grad, kv_grad,
+    *scratch,
+):
+    *buffers, kv_own, norm_mine, slots, column, sq_mine, sq_slots, sq_column, send_sems, recv_sems = scratch
+    p = Place(groups, seqs)
+    rows, width = x_ref.shape
+    local = rows // SPAN
+    spans = local * seqs
+    length, first_span = info_ref[0], info_ref[1]
+    meet(p)
+    copies = Copies(send_sems, recv_sems)
+
+    def scatter(grad, at, out):
+        return scatter_steps(p, copies, grad, *buffers[5 * at : 5 * at + 5], out)
+
+    out_down, out_pu = scatter(down_ref, 0, down_out), scatter(pu_ref, 1, pu_out)
+    tick(out_down, out_pu)
+    kt_scr[...] = summ_ref[:, :width].T
+    dsumm_scr[...] = jnp.zeros_like(dsumm_scr)
+
+    def attend_back(at, index):
+        caps = span_caps(length, first_span + index)
+        attend_back_span(
+            mixed_ref, grad_ref, at, width, summ_ref, kt_scr, caps,
+            lambda pair: lse_ref[index, pair : pair + 1, :], mg_scr, dkv_scr, at, dsumm_scr,
+        )
+
+    for part in range(4):
+        tiles(part * local // 4, (part + 1) * local // 4, SPAN, attend_back)
+        tick(out_down if part % 2 == 0 else out_pu)
+    swap = []
+    for z in range(p.chips):
+        block = dsumm_scr.at[pl.ds(pl.multiple_of((2 * z + p.other) * local, local), local)]
+        swap.append(copies.start(block, dsumm_got.at[z], p.sibling()))
+    tile = 256
+    count = rows // tile
+    gain, shift = norms_ref[0:1, :], norms_ref[1:2, :]
+
+    def recompute(at, index):
+        xhat, _ = normalize(x_ref[pl.ds(at, tile), :].astype(F32))
+        n1t_scr[:, pl.ds(at, tile)] = (xhat * gain + shift).astype(BF).T
+
+    tiles(0, count, tile, recompute)
+    for copy in swap:
+        copy.wait_recv()
+
+    def half_sum(z):
+        mine = dsumm_scr[pl.ds(pl.multiple_of((2 * z + p.c) * local, local), local), :]
+        return mine + dsumm_got[z]
+
+    along = []
+    for k in range(1, p.chips):
+        to = p.along(k)
+        dsumm_low[k - 1] = half_sum(to).astype(BF)
+        along.append(copies.start(dsumm_low.at[k - 1], dsumm_last.at[k - 1], p.at(p.b, to, p.c)))
+    per_block = n1t_scr.shape[0] // (groups * seqs)
+
+    def weight_grad(into, begin, size):
+        block = dot(n1t_scr[...], mg_scr[:, begin : begin + size]).astype(BF)
+        return block.reshape(groups, p.chips, 2, per_block, size)
+
+    cols = 256
+    for at in range(0, width, cols):
+        q_grad[:, :, :, :, at : at + cols] = weight_grad(q_grad, at, cols)
+    out_q = scatter(q_grad, 2, qkv_out.at[:, :width])
+    tick(out_q, out_down, out_pu)
+
+    def back_q(at, index):
+        input_grad_ref[pl.ds(at, tile), :] = dot_nt(mg_scr[pl.ds(at, tile), :width], weight_ref[:, :width])
+
+    tiles(0, count, tile, back_q)
+    total = half_sum(p.z)
+    for k, copy in enumerate(along):
+        copy.wait_recv()
+        total = total + dsumm_last[k].astype(F32)
+    extra_scr[...] = total
+    tick(out_down)
+
+    def add_extra(at, index):
+        begin = (first_span + index) * SPAN
+        extra = extra_scr[pl.ds(index, 1), :]
+        extra = extra * span_scale(length, begin, extra.shape)
+        here = dkv_scr[pl.ds(at, SPAN), :]
+        pos = lax.broadcasted_iota(jnp.int32, here.shape, 0)
+        mg_scr[pl.ds(at, SPAN), width:] = (here + jnp.where(pos < length - begin, extra, 0.0)).astype(BF)
+
+    tiles(0, local, SPAN, add_extra)
+    for at in range(0, 2 * width, cols):
+        kv_grad[:, :, :, :, at : at + cols] = weight_grad(kv_grad, width + at, cols)
+    out_kv = scatter(kv_grad, 3, kv_own)
+    tick(out_kv, out_q, out_pu, out_down)
+    norm_mine[0:2, :] = jnp.zeros_like(norm_mine[0:2, :])
+    norm_mine[2:4, :] = norm_two_ref[...]
+
+    def finish(at, index):
+        here = pl.ds(at, tile)
+        xhat, rstd = normalize(x_ref[here, :].astype(F32))
+        back = input_grad_ref[here, :] + dot_nt(mg_scr[here, width:], weight_ref[:, width:])
+        input_grad_ref[here, :] = resid_grad_ref[here, :] + norm_back(back, gain, xhat, rstd)
+        norm_mine[0:1, :] += jnp.sum(back * xhat, axis=0, keepdims=True)
+        norm_mine[1:2, :] += jnp.sum(back, axis=0, keepdims=True)
+
+    for part in range(4):
+        tiles(part * count // 4, (part + 1) * count // 4, tile, finish)
+        tick(out_kv, out_q, out_pu, out_down)
+    norm_sum = share_sum_steps(p, copies, norm_mine, slots, column, norm_out)
+    run_all(norm_sum, out_kv, out_q, out_pu, out_down)
+    qkv_out[:, width:] = kv_own[...]
+    local_sum = sum(jnp.sum(jnp.square(out[...]), keepdims=True) for out in (qkv_out, pu_out, down_out))
+    sq_mine[...] = jnp.broadcast_to(local_sum, sq_mine.shape)
+    run_all(share_sum_steps(p, copies, sq_mine, sq_slots, sq_column, total_out))
+    total_out[...] = total_out[...] + jnp.sum(jnp.square(norm_out[...]), keepdims=True)
+    copies.finish()
+
+
+FRONT_COPIES = 4 * GATHER_COPIES + 8
+BACK_COPIES = 4 * SCATTER_COPIES + 2 * SHARE_COPIES + 8
 
 
 def qkv_kernel(info_ref, x_ref, norms_ref, weight_ref, mixed_ref, summ_ref, sum_scr):
@@ -644,9 +816,10 @@
 PARAMS = pltpu.CompilerParams(vmem_limit_bytes=VMEM_LIMIT)
 
 
-def remote_call(kernel, groups, seqs, name, collective_id, out_shape, scratch, copies):
+def remote_call(kernel, groups, seqs, name, collective_id, out_shape, scratch, copies, in_specs):
     return pl.pallas_call(
         functools.partial(kernel, groups, seqs),
+        in_specs=in_specs,
         out_shape=out_shape,
         scratch_shapes=list(scratch)
         + [pltpu.SemaphoreType.DMA((copies,)), pltpu.SemaphoreType.DMA((copies,))],
@@ -685,66 +858,13 @@
     return (*reduced, norm_total, jnp.broadcast_to(squares, (8, LANES)))
 
 
-def body(groups, seqs, inputs, out_grad, lengths, *state):
+def mlp_call(x, attn_out, grad_rows, norms, pu_full, down_full):
     sds = jax.ShapeDtypeStruct
-    rows, width = inputs.shape[1], inputs.shape[2]
-    own_rows, down_rows = state[0].shape[0], state[3].shape[0]
-    hidden = state[2].shape[1]
-    chips = seqs // 2
-    direct = groups == 4 and seqs % 4 == 0 and own_rows % 16 == 0
-    grid3 = (groups, chips, 2)
-    if direct:
-        qkv_full, pu_full, down_full, norms = remote_call(
-            gather_kernel, groups, seqs, "gather", 0,
-            [
-                sds((*grid3, own_rows, 3 * width), BF), sds((*grid3, own_rows, width + hidden), BF),
-                sds((*grid3, down_rows, width), BF), sds((4, width), F32),
-            ],
-            [pltpu.VMEM((*grid3, 4, LANES), F32)], 4 * GATHER_COPIES,
-        )(*state[:5])
-        qkv_full = qkv_full.reshape(width, 3 * width)
-        pu_full = pu_full.reshape(width, width + hidden)
-        down_full = down_full.reshape(hidden, width)
-    else:
-        qkv_full, pu_full, down_full, norms = gather_plain(state[:5])
-    local = rows // SPAN
-    spans = local * seqs
-    first_span = lax.axis_index("seq") * local
-    length = lengths[0]
-    info = jnp.stack([length, first_span.astype(jnp.int32)])
-    x, grad_rows = inputs[0], out_grad[0]
+    rows, width = x.shape
+    hidden = down_full.shape[0]
     tile = 256
     steps = rows // tile
-    mixed, own_summ = pl.pallas_call(
-        qkv_kernel,
-        grid=(steps,),
-        in_specs=[SCALARS, by_rows(tile, width), whole(norms.shape), whole(qkv_full.shape)],
-        out_specs=[by_rows(tile, 3 * width), whole((local, 2 * width))],
-        out_shape=[sds((rows, 3 * width), BF), sds((local, 2 * width), BF)],
-        scratch_shapes=[pltpu.VMEM((local, 2 * width), F32)],
-        compiler_params=PARAMS,
-        name="qkv",
-    )(info, x, norms, qkv_full)
-    if direct:
-        summ = remote_call(
-            summary_gather_kernel, groups, seqs, "summary_gather", 1,
-            sds((chips, 2, local, 2 * width), BF), [], 2 * chips,
-        )(own_summ).reshape(spans, 2 * width)
-    else:
-        summ = lax.all_gather(own_summ, "seq", axis=0, tiled=True)
-    pairs = width // LANES
-    lse_spec = pl.BlockSpec((1, pairs, 2 * SPAN), lambda i: (i, 0, 0))
-    attn_out, lse = pl.pallas_call(
-        attend_kernel,
-        grid=(local,),
-        in_specs=[SCALARS, by_rows(SPAN, 3 * width), whole(summ.shape)],
-        out_specs=[by_rows(SPAN, width), lse_spec],
-        out_shape=[sds((rows, width), BF), sds((local, pairs, 2 * SPAN), F32)],
-        scratch_shapes=[pltpu.VMEM((width, spans), BF)],
-        compiler_params=PARAMS,
-        name="attend",
-    )(info, mixed, summ)
-    outputs, resid_grad, attn_grad, pu_grad, down_grad, norm_two = pl.pallas_call(
+    return pl.pallas_call(
         mlp_kernel,
         grid=(steps,),
         in_specs=[by_rows(tile, width)] * 3
@@ -763,6 +883,104 @@
         compiler_params=PARAMS,
         name="mlp",
     )(x, attn_out, grad_rows, norms, pu_full, down_full)
+
+
+def direct_body(groups, seqs, inputs, out_grad, lengths, *state):
+    sds = jax.ShapeDtypeStruct
+    rows, width = inputs.shape[1], inputs.shape[2]
+    own_rows, down_rows = state[0].shape[0], state[3].shape[0]
+    hidden = state[2].shape[1]
+    chips = seqs // 2
+    grid3 = (groups, chips, 2)
+    local = rows // SPAN
+    spans = local * seqs
+    pairs = width // LANES
+    info = jnp.stack([lengths[0], (lax.axis_index("seq") * local).astype(jnp.int32)])
+    x, grad_rows = inputs[0], out_grad[0]
+    scalars_first = lambda n: [SCALARS] + [pl.BlockSpec(memory_space=pltpu.VMEM)] * n
+    qkv_full, pu_full, down_full, norms, mixed, summ, attn_out, lse = remote_call(
+        front_kernel, groups, seqs, "front", 0,
+        [
+            sds((*grid3, own_rows, 3 * width), BF), sds((*grid3, own_rows, width + hidden), BF),
+            sds((*grid3, down_rows, width), BF), sds((4, width), F32), sds((rows, 3 * width), BF),
+            sds((chips, 2, local, 2 * width), BF), sds((rows, width), BF),
+            sds((local, pairs, 2 * SPAN), F32),
+        ],
+        [
+            pltpu.VMEM((*grid3, 4, LANES), F32), pltpu.VMEM((rows, width), F32),
+            pltpu.VMEM((local, 2 * width), F32), pltpu.VMEM((width, spans), BF),
+        ],
+        FRONT_COPIES, scalars_first(6),
+    )(info, x, *state[:5])
+    qkv_full = qkv_full.reshape(width, 3 * width)
+    outputs, resid_grad, attn_grad, pu_grad, down_grad, norm_two = mlp_call(
+        x, attn_out, grad_rows, norms, pu_full.reshape(width, width + hidden), down_full.reshape(hidden, width)
+    )
+    shapes = ((down_rows, width), (own_rows, width + hidden), (own_rows, width), (own_rows, 2 * width))
+    scratch = [
+        pltpu.VMEM((rows, 3 * width), BF), pltpu.VMEM((rows, 2 * width), F32), pltpu.VMEM((width, rows), BF),
+        pltpu.VMEM((width, spans), BF), pltpu.VMEM((spans, 2 * width), F32),
+        pltpu.VMEM((chips, local, 2 * width), F32), pltpu.VMEM((chips - 1, local, 2 * width), BF),
+        pltpu.VMEM((chips - 1, local, 2 * width), BF), pltpu.VMEM((local, 2 * width), F32),
+        pltpu.VMEM((*grid3, own_rows, width), BF), pltpu.VMEM((*grid3, own_rows, 2 * width), BF),
+    ]
+    scratch += [buffer for shape in shapes for buffer in scatter_scratch(groups, chips, *shape)]
+    scratch += [
+        pltpu.VMEM((own_rows, 2 * width), F32),
+        pltpu.VMEM((4, width), F32), pltpu.VMEM((6, 4, width), F32), pltpu.VMEM((chips, 4, width), F32),
+        pltpu.VMEM((8, LANES), F32), pltpu.VMEM((6, 8, LANES), F32), pltpu.VMEM((chips, 8, LANES), F32),
+    ]
+    input_grad, *grads, norm_total, total = remote_call(
+        back_kernel, groups, seqs, "back", 1,
+        [
+            sds((rows, width), F32), sds((own_rows, 3 * width), F32), sds((own_rows, width + hidden), F32),
+            sds((down_rows, width), F32), sds((4, width), F32), sds((8, LANES), F32),
+        ],
+        scratch, BACK_COPIES, scalars_first(11),
+    )(
+        info, x, mixed, attn_grad, lse, summ.reshape(spans, 2 * width), resid_grad,
+        pu_grad.reshape(*grid3, own_rows, width + hidden), down_grad.reshape(*grid3, down_rows, width),
+        norms, qkv_full, norm_two,
+    )
+    return outputs, input_grad, grads, norm_total, total
+
+
+def plain_body(groups, seqs, inputs, out_grad, lengths, *state):
+    sds = jax.ShapeDtypeStruct
+    rows, width = inputs.shape[1], inputs.shape[2]
+    qkv_full, pu_full, down_full, norms = gather_plain(state[:5])
+    local = rows // SPAN
+    spans = local * seqs
+    info = jnp.stack([lengths[0], (lax.axis_index("seq") * local).astype(jnp.int32)])
+    x, grad_rows = inputs[0], out_grad[0]
+    tile = 256
+    steps = rows // tile
+    mixed, own_summ = pl.pallas_call(
+        qkv_kernel,
+        grid=(steps,),
+        in_specs=[SCALARS, by_rows(tile, width), whole(norms.shape), whole(qkv_full.shape)],
+        out_specs=[by_rows(tile, 3 * width), whole((local, 2 * width))],
+        out_shape=[sds((rows, 3 * width), BF), sds((local, 2 * width), BF)],
+        scratch_shapes=[pltpu.VMEM((local, 2 * width), F32)],
+        compiler_params=PARAMS,
+        name="qkv",
+    )(info, x, norms, qkv_full)
+    summ = lax.all_gather(own_summ, "seq", axis=0, tiled=True)
+    pairs = width // LANES
+    lse_spec = pl.BlockSpec((1, pairs, 2 * SPAN), lambda i: (i, 0, 0))
+    attn_out, lse = pl.pallas_call(
+        attend_kernel,
+        grid=(local,),
+        in_specs=[SCALARS, by_rows(SPAN, 3 * width), whole(summ.shape)],
+        out_specs=[by_rows(SPAN, width), lse_spec],
+        out_shape=[sds((rows, width), BF), sds((local, pairs, 2 * SPAN), F32)],
+        scratch_shapes=[pltpu.VMEM((width, spans), BF)],
+        compiler_params=PARAMS,
+        name="attend",
+    )(info, mixed, summ)
+    outputs, resid_grad, attn_grad, pu_grad, down_grad, norm_two = mlp_call(
+        x, attn_out, grad_rows, norms, pu_full, down_full
+    )
     dq, dkv, dsumm = pl.pallas_call(
         attend_back_kernel,
         grid=(local,),
@@ -773,18 +991,7 @@
         compiler_params=PARAMS,
         name="attend_back",
     )(info, mixed, attn_grad, lse, summ)
-    if direct:
-        block = (local, 2 * width)
-        extra = remote_call(
-            summary_scatter_kernel, groups, seqs, "summary_scatter", 2, sds(block, F32),
-            [
-                pltpu.VMEM((chips, *block), F32), pltpu.VMEM((chips - 1, *block), BF),
-                pltpu.VMEM((chips - 1, *block), BF),
-            ],
-            chips,
-        )(dsumm.reshape(chips, 2, *block))
-    else:
-        extra = lax.psum_scatter(dsumm, "seq", scatter_dimension=0, tiled=True)
+    extra = lax.psum_scatter(dsumm, "seq", scatter_dimension=0, tiled=True)
     input_grad, qkv_grad, norm_one = pl.pallas_call(
         final_kernel,
         grid=(steps,),
@@ -801,25 +1008,16 @@
         name="final",
     )(info, x, dq, dkv, extra, resid_grad, norms, qkv_full)
     norm_grad = jnp.concatenate([norm_one, norm_two], axis=0)
-    if direct:
-        shapes = ((down_rows, width), (own_rows, width + hidden), (own_rows, 3 * width))
-        scratch = [buffer for shape in shapes for buffer in scatter_scratch(groups, chips, *shape)]
-        scratch += [
-            pltpu.VMEM((6, 4, width), F32), pltpu.VMEM((chips, 4, width), F32),
-            pltpu.VMEM((8, LANES), F32), pltpu.VMEM((6, 8, LANES), F32), pltpu.VMEM((chips, 8, LANES), F32),
-        ]
-        reduced = remote_call(
-            reduce_kernel, groups, seqs, "reduce", 3,
-            [sds(shape, F32) for shape in (*reversed(shapes), (4, width), (8, LANES))],
-            scratch, 3 * SCATTER_COPIES + 2 * SHARE_COPIES,
-        )(
-            qkv_grad.reshape(*grid3, own_rows, 3 * width),
-            pu_grad.reshape(*grid3, own_rows, width + hidden),
-            down_grad.reshape(*grid3, down_rows, width), norm_grad,
-        )
-    else:
-        reduced = reduce_plain(qkv_grad, pu_grad, down_grad, norm_grad)
-    *grads, norm_total, total = reduced
+    *grads, norm_total, total = reduce_plain(qkv_grad, pu_grad, down_grad, norm_grad)
+    return outputs, input_grad, grads, norm_total, total
+
+
+def body(groups, seqs, *args):
+    state = args[3:]
+    direct = groups == 4 and seqs % 4 == 0 and state[0].shape[0] % 16 == 0
+    run = direct_body if direct else plain_body
+    outputs, input_grad, grads, norm_total, total = run(groups, seqs, *args)
+    sds = jax.ShapeDtypeStruct
     index = lax.axis_index("batch") * seqs + lax.axis_index("seq")
     owned = [sds(w.shape, F32) for w in state[:5]]
     grad_norm, *fresh, shift_clipped = pl.pallas_call(

time: 264 us -> 217 us (0.82)
  Pallas kernels: 260 us -> 210 us
  local copies, waits for them, and re-layouts: 0.01 us -> 4.64 us
    pallas_call x9 -> x3, Pallas kernels: 257 us -> 207 us  [the longest x1 94.4 us: direct_body(): remote_call(back_kernel, groups, seqs, 'back', 1, [sds((rows, width), F32...]
    unnamed x2 -> x1, local copies, waits for them, and re-layouts: 0.01 us -> 4.64 us
where the time goes in v3:
time: 217 us
  Pallas kernels  210 us (97%)
  local copies, waits for them, and re-layouts  4.64 us (2%)
    pallas_call x1, Pallas kernels, direct_body(): remote_call(back_kernel, groups, seqs, 'back', 1, [sds((rows, width), F32...  94.4 us
    pallas_call x1, Pallas kernels, direct_body(): remote_call(front_kernel, groups, seqs, 'front', 0, [sds((*grid3, own_row...  64.5 us
    pallas_call x1, Pallas kernels, mlp_call(): pl.pallas_call(mlp_kernel, grid=(steps,), in_specs=[by_rows(tile, width)]...  48.3 us
    unnamed x1, local copies, waits for them, and re-layouts  4.64 us

profile of v3, /device:TPU:0, one launch (start us, length us, event | category | flops | bytes accessed | tf_op | source)
XLA Modules:
  0.0 216.5 jit_solution(5516200517041840862)
XLA Ops:
  1.3 0.6 pad_add_fusion.info_ref
  1.9 64.5 %front.1 = (bf16[4,4,2,16,1536]{4,3,2,1,0:T(8,128)(2,1)}, bf16[4,4,2,16,2560]{4,3,2,1,0:T(8,128)(2,1)}, bf16[4,4,2,64,512]{4,3,2,1,0:T(8,128)(2,1)}, f32[4,512]{...) custom-call(s32[2]{0:T(128)} %pad_add_fusion.info_ref, ...), custom_call_target="tpu_custom_call" | custom-call | tf_op jit(solution)/shard_map/front/pallas_call | solution.py:901
  66.4 48.3 %mlp.1 = (bf16[2048,512]{1,0:T(8,128)(2,1)}, f32[2048,512]{1,0:T(8,128)}, bf16[2048,512]{1,0:T(8,128)(2,1)}, bf16[512,2560]{1,0:T(8,128)(2,1)}, bf16[2048,512]{1,0:T(8,128)(2,1)}, /*index=5*/f32[2,512]{1,0:T(2,128)}) custom-call(bf16[2048,512]{1,0:T(8,128)(2,1)} %bitcast.15, bf16[2048,512]{1,0:T(8,128)(2,1)} %get-tuple-element.56.attn_ref, ...), custom_call_target="tpu_custom_call" | custom-call | tf_op jit(solution)/shard_map/mlp/pallas_call | solution.py:867
  114.7 94.4 %back.1 = (f32[2048,512]{1,0:T(8,128)}, f32[16,1536]{1,0:T(8,128)}, f32[16,2560]{1,0:T(8,128)}, f32[64,512]{1,0:T(8,128)}, f32[4,512]{1,0:T(4,128)}, /*index=5*/f32[8,128]{1,0:T(8,128)}) custom-call(s32[2]{0:T(128)} %pad_add_fusion.info_ref, bf16[2048,512]{1,0:T(8,128)(2,1)} %bitcast.16, bf16[2048,1536]{1,0:T(8,128)(2,1)} %get-tuple-element.61.mixed_ref, ...), custom_call_target="tpu_custom_call" | custom-call | tf_op jit(solution)/shard_map/back/pallas_call | solution.py:933
  209.1 2.8 %update.1 = (f32[1,1]{1,0:T(1,128)}, f32[16,1536]{1,0:T(8,128)}, f32[16,512]{1,0:T(8,128)}, f32[16,2048]{1,0:T(8,128)}, f32[64,512]{1,0:T(8,128)}, /*index=5*/f3...) custom-call(s32[1]{0:T(128)} %bitcast.11.index_ref, ...), custom_call_target="tpu_custom_call" | custom-call | tf_op jit(solution)/shard_map/update/pallas_call | solution.py:1023
  211.9 4.6 %copy.39 = f32[1,2048,512]{2,1,0:T(8,128)} copy(f32[1,2048,512]{2,1,0:T(8,128)} %bitcast.17) | data formatting | bytes 8388608
